TPU v7x, 512 devices: a whole 4x4x16 slice. The times are simulated.
512 devices in a mesh: tok: 8 (over y, core), voc: 16 (over z), tp: 4 (over x).
Axes of the slice: x: 4, y: 4, z: 16, core: 2. Of those that a mesh axis runs over, the one named last changes fastest.
Arguments:
- hidden: bfloat16 [512, 7168], P(('tok', 'voc'), 'tp'), may hold values from -8 to 8
- head_weight: bfloat16 [7168, 65536], P('tp', ('tok', 'voc')), may hold values from -1 to 1
- targets: int32 [512], replicated, may hold values from 0 to 65535
- offsets: int32 [32], replicated, may hold values from 1 to 511, as said below
- lengths: int32 [32], replicated, may hold values from 1 to 128
- group_ids: int32 [32], replicated, may hold values from 0 to 1, as said below
- rewards: float32 [32], replicated, may hold values from -4 to 4
Outputs:
- hidden_grad: bfloat16 [512, 7168], P(('tok', 'voc'), 'tp')
- policy_loss: float32 [], replicated
Inputs may be any that keep to these rules, and one draw needn't show every extreme that they name: Rollouts lie packed in order over the 512 rows; the response of rollout i occupies rows offsets[i] to offsets[i] + lengths[i] - 1, ends that rollout and follows at least one prompt row of it; responses are disjoint and hold exactly 256 rows in all. `group_ids`: each of the 2 groups holds exactly 16 rollouts.
All inputs are finite; a program needn't handle non-finite values.
Results may differ from a plain program's by a relative error of at most 0.0054.
Values may be sent and summed in bfloat16 or wider, within the bound.
No kernel may reach another device: no remote copies, remote signals or barrier semaphores. Data moves between devices by JAX's collectives and lax.ppermute only.
A program may use at most 64 MiB of HBM per device.

v0:
```python
import jax
import jax.numpy as jnp
from jax import lax
from jax.sharding import PartitionSpec as P

GROUP_SIZE = 16
GROUPS = 2


entropy_weight = 0.2


def per_device(hidden, head_weight, targets, offsets, lengths, group_ids, rewards):
    total_rows = targets.shape[0]
    vocab_local = head_weight.shape[1]
    row_index = jnp.arange(total_rows, dtype=jnp.int32)
    response_end = offsets + lengths
    member = (
        (row_index[:, None] >= offsets[None, :]) & (row_index[:, None] < response_end[None, :])
    ).astype(jnp.float32)
    live_rows = jnp.sum(member, axis=1)
    grouping = (group_ids[:, None] == jnp.arange(GROUPS, dtype=jnp.int32)[None, :]).astype(
        jnp.float32
    )
    group_mean = jnp.sum(rewards[:, None] * grouping, axis=0) / GROUP_SIZE
    advantage = rewards - jnp.sum(grouping * group_mean[None, :], axis=1)
    row_advantage = jnp.sum(member * advantage[None, :], axis=1)
    weight_all = total_rows / jnp.sum(lengths).astype(jnp.float32)
    device_place = lax.axis_index("tok") * lax.axis_size("voc") + lax.axis_index("voc")
    vocab_first = device_place * vocab_local
    partial_logits = jnp.dot(
        lax.all_gather(hidden, ("tok", "voc"), axis=0, tiled=True),
        head_weight,
        preferred_element_type=jnp.float32,
    )
    logits = lax.psum(partial_logits, "tp")
    own_target = jnp.take(targets, row_index)
    own_live = jnp.take(live_rows, row_index)
    own_advantage = jnp.take(row_advantage, row_index)
    columns = vocab_first + jnp.arange(vocab_local, dtype=jnp.int32)
    target_hit = columns[None, :] == own_target[:, None]
    target_local = jnp.sum(jnp.where(target_hit, logits, 0.0), axis=1)
    local_top = jnp.max(logits, axis=1)
    row_top = lax.pmax(local_top, ("tok", "voc"))
    shifted = jnp.exp(logits - row_top[:, None])
    total_exp, total_weighted, target_value = lax.psum(
        (jnp.sum(shifted, axis=1), jnp.sum(shifted * logits, axis=1), target_local), ("tok", "voc")
    )
    log_total = row_top + jnp.log(total_exp)
    entropy = log_total - total_weighted / total_exp
    probability = jnp.exp(logits - log_total[:, None])
    row_weight = weight_all * own_live
    grad_logits = row_weight[:, None] * (
        own_advantage[:, None] * (probability - target_hit.astype(jnp.float32))
        + entropy_weight * probability * (logits - log_total[:, None] + entropy[:, None])
    )
    grad_logits = grad_logits.astype(jnp.bfloat16)
    row_loss = own_live * (-own_advantage * (target_value - log_total) - entropy_weight * entropy)
    local_loss = weight_all * jnp.sum(row_loss)
    hidden_grad = lax.psum_scatter(
        lax.dot_general(
            grad_logits, head_weight, (((1,), (1,)), ((), ())), preferred_element_type=jnp.float32
        ),
        ("tok", "voc"),
        scatter_dimension=0,
        tiled=True,
    )
    return (hidden_grad.astype(jnp.bfloat16), local_loss)


def solution(mesh):
    placed = (P(("tok", "voc"), "tp"), P("tp", ("tok", "voc")), P(), P(), P(), P(), P())
    return jax.shard_map(
        per_device,
        mesh=mesh,
        in_specs=placed,
        out_specs=(P(("tok", "voc"), "tp"), P()),
        check_vma=False,
    )
```

profile of v0, /device:TPU:2, one launch (start us, length us, event | category | flops | bytes accessed | tf_op | source)
XLA Modules:
  0.0 1272.6 jit_solution(3426125876499586220)
XLA Ops:
  7.2 0.0 copy-start
  7.2 0.0 all-gather.3.cloned.1.call-start
  7.2 0.7 all-gather.3.cloned.1.call-update
  7.9 0.0 all-reduce.6.cloned.1.call-start
  8.0 0.8 select_reduce_fusion.2
  8.7 146.2 %all-gather.3.cloned.1.call-done = bf16[128,4,1792]{2,1,0:T(4,128)(2,1)} async-done(((bf16[1,4,1792]{2,1,0:T(4,128)(2,1)}), bf16[128,4,1792]{2,1,0:T(4,128)(2,1)}) %all-gather.3.cloned.1.call-update) | async-done | bytes 1835024 | tf_op jit(solution)/shard_map/all_gather | solution.py:32
  155.0 3.9 reshape.63
  158.9 0.0 copy-done
  158.9 3.6 fusion.19
  162.6 0.0 all-reduce.6.cloned.1.call-update
  162.6 0.0 copy-done.5
  162.6 0.1 select_reduce_fusion.1
  162.7 0.0 copy-done.6
  162.7 0.5 copy-done.1
  163.2 3.5 gather_fusion
  166.7 0.0 copy-done.3
  166.7 0.0 copy-done.4
  166.7 0.6 fusion.18
  167.4 0.1 convert_reduce_fusion
  167.5 3.5 gather_fusion.1
  171.0 3.5 gather_fusion.2
  175.2 1.3 dynamic-slice
  177.1 42.6 %all-reduce.6.cloned.1.call-done = f32[512,512]{1,0:T(8,128)} async-done(((f32[512,512]{1,0:T(8,128)}), f32[512,512]{1,0:T(8,128)}) %all-reduce.6.cloned.1.call-update) | async-done | bytes 1048592 | tf_op jit(solution)/shard_map/psum | solution.py:36
  219.7 1.5 reduce_max.9
  221.2 251.0 %pmax.7 = f32[512]{0:T(512)S(1)} all-reduce(f32[512]{0:T(512)S(1)} %reduce_max.9), channel_id=1, replica_groups=mesh['tok'=8,'voc'=16,'tp'=4] {'tok','voc'}, use_global_device_ids=true, to_apply=%region_7.9 | all-reduce | flops 512 | bytes 4096 | tf_op jit(solution)/shard_map/pmax | solution.py:44
  472.2 1.8 multiply_reduce_fusion
  474.0 246.9 %all-reduce.2 = (f32[512]{0:T(512)S(1)}, f32[512]{0:T(512)S(1)}) all-reduce(f32[512]{0:T(512)S(1)} %get-tuple-element.4, f32[512]{0:T(512)S(1)} %get-tuple-element.3), channel_id=1, replica_groups=mesh['tok'=8,'voc'=16,'tp'=4] {'tok','voc'}, use_global_device_ids=true, to_apply=%region_9.11 | all-reduce | flops 1024 | bytes 8192 | tf_op jit(solution)/shard_map/psum | solution.py:46
  720.9 0.0 copy-done.2
  720.9 3.3 fusion.7
  724.2 537.9 %all-reduce.7 = (bf16[512,1792]{1,0:T(8,128)(2,1)}, f32[512]{0:T(512)S(1)}) all-reduce(f32[512,1792]{1,0:T(8,128)} %fusion.7, f32[512]{0:T(512)S(1)} %get-tuple-element.5), channel_id=2, replica_groups=mesh['tok'=8,'voc'=16,'tp'=4] {'tok','voc'}, use_global_device_ids=true, to_apply=%region_12.14.clone | all-reduce | flops 918016 | bytes 5509120
  1262.1 0.6 multiply_reduce_fusion.1
  1263.3 1.4 dynamic-slice_convert_fusion
  (13 shorter events, 0.1 us)
Async XLA Ops:
  7.2 151.8 %copy-start = (bf16[1792,512]{1,0:T(8,128)(2,1)S(1)}, bf16[1792,512]{1,0:T(8,128)(2,1)}, u32[]{:S(2)}) copy-start(bf16[1792,512]{1,0:T(8,128)(2,1)} %param.10) | copy-start | bytes 5505028
  7.2 147.8 %all-gather.3.cloned.1.call-start = ((), (), s32[]{:S(2)}) async-start(), calls=%async_computation.1 | async-start | bytes 1849344 | tf_op jit(solution)/shard_map/all_gather | solution.py:32
  7.9 211.8 %all-reduce.6.cloned.1.call-start = ((), (), s32[]{:S(2)}) async-start(), calls=%async_computation | async-start | bytes 2097152 | tf_op jit(solution)/shard_map/psum | solution.py:36
  158.9 3.7 copy-start.5
  158.9 3.8 copy-start.6
  162.5 0.7 copy-start.1
  162.5 4.2 copy-start.3
  162.5 4.2 copy-start.4
  219.7 501.2 %copy-start.2 = (f32[512,512]{1,0:T(8,128)S(1)}, f32[512,512]{1,0:T(8,128)}, u32[]{:S(2)}) copy-start(f32[512,512]{1,0:T(8,128)} %all-reduce.6.cloned.1.call-done) | copy-start | bytes 3145732
Sparse Core Ops, SparseCore 0:
  11.0 143.8 all-gather.2
  162.7 56.9 all-reduce.5
where the time goes:
time: 1270 us
  blocking collectives  1040 us (82%)
  waiting for transfers between devices  190 us (15%)
  local copies, waits for them, and re-layouts  17.6 us (1%)
  between operations  17.3 us (1%)
    unnamed x1, blocking collectives  538 us
    pmax x1, blocking collectives, per_device(): row_top = lax.pmax(local_top, ('tok', 'voc'))  251 us
    psum x1, blocking collectives, per_device(): lax.psum((jnp.sum(shifted, axis=1), jnp.sum(shifted * logits, axis=1), ta...  247 us
    all_gather x1, waiting for transfers between devices, per_device(): lax.all_gather(hidden, ('tok', 'voc'), axis=0, tiled=True)  146 us
    psum x1, waiting for transfers between devices, per_device(): logits = lax.psum(partial_logits, 'tp')  42.6 us
  transfers between devices with their start and end apart: 2, of which 2 were waited for; matrix products, arithmetic and copies ran while one was open for 1% of the time, Pallas kernels for 0%

commit v1 on v0

v1 whole, which is shorter than its diff:
```python
import jax
import jax.numpy as jnp
from jax import lax
from jax.sharding import Mesh, PartitionSpec as P

GROUP_SIZE = 16
GROUPS = 2
ENTROPY_WEIGHT = 0.2
Y, C, Z, X = 4, 2, 16, 4


def combine(stats):
    top = jnp.max(stats[:, 0], axis=0)
    scale = jnp.exp(stats[:, 0] - top[None])
    total = jnp.sum(scale * stats[:, 1], axis=0)
    weighted = jnp.sum(scale * (stats[:, 2] + (stats[:, 0] - top[None]) * stats[:, 1]), axis=0)
    target = jnp.sum(stats[:, 3], axis=0)
    return jnp.stack([top, total, weighted, target])


def spread(block, axes, n):
    sent = jnp.broadcast_to(block[None], (n, *block.shape))
    return lax.all_to_all(sent, axes, 0, 0, tiled=True)


def per_device(hidden, head_weight, targets, offsets, lengths, group_ids, rewards):
    y, c, z, x = (lax.axis_index(a) for a in ("y", "c", "z", "x"))
    depth, vocab = head_weight.shape
    total_rows = targets.shape[0]
    other_weight = lax.ppermute(head_weight, "c", [(0, 1), (1, 0)])

    rows = total_rows // C
    place = jnp.arange(rows, dtype=jnp.int32)
    per_tok = total_rows // (Y * C)
    row_index = (2 * (place // per_tok) + c) * per_tok + place % per_tok
    member = (
        (row_index[None, :] >= offsets[:, None])
        & (row_index[None, :] < (offsets + lengths)[:, None])
    ).astype(jnp.float32)
    live = jnp.sum(member, axis=0)
    grouping = (group_ids[:, None] == jnp.arange(GROUPS, dtype=jnp.int32)[None, :]).astype(jnp.float32)
    group_mean = jnp.sum(rewards[:, None] * grouping, axis=0) / GROUP_SIZE
    advantage = rewards - jnp.sum(grouping * group_mean[None, :], axis=1)
    row_advantage = jnp.sum(member * advantage[:, None], axis=0)
    weight_all = total_rows / jnp.sum(lengths).astype(jnp.float32)
    own_targets = targets.reshape(Y, C, per_tok)[:, c].reshape(rows)

    tok_rows = spread(hidden, "z", Z).reshape(per_tok, depth)
    my_rows = lax.all_gather(tok_rows, "y", axis=0, tiled=True)

    contract = (((0,), (1,)), ((), ()))
    part = jnp.concatenate(
        [
            lax.dot_general(w, my_rows, contract, preferred_element_type=jnp.float32)
            for w in (head_weight, other_weight)
        ]
    )
    chunk = C * vocab // X
    part = lax.all_to_all(part.reshape(X, chunk, rows), "x", 0, 0, tiled=True)
    logits = jnp.sum(part, axis=0)

    first = x * chunk
    core = jnp.where(first < vocab, c, 1 - c)
    first_column = ((2 * y + core) * Z + z) * vocab + first % vocab
    hit = (first_column + jnp.arange(chunk, dtype=jnp.int32))[:, None] == own_targets[None, :]
    top = jnp.max(logits, axis=0)
    shifted = logits - top[None]
    e = jnp.exp(shifted)
    stats = jnp.stack(
        [top, jnp.sum(e, 0), jnp.sum(e * shifted, 0), jnp.sum(jnp.where(hit, logits, 0.0), 0)]
    )
    stats = combine(spread(stats, "z", Z))
    top, total, weighted, target_value = combine(spread(stats, ("y", "x"), Y * X))
    log_sum = jnp.log(total)
    log_total = top + log_sum
    entropy = log_sum - weighted / total
    row_loss = live * (-row_advantage * (target_value - log_total) - ENTROPY_WEIGHT * entropy)
    loss = jnp.sum(row_loss)
    loss = weight_all * (loss + lax.ppermute(loss, "c", [(0, 1), (1, 0)]))

    log_probability = logits - log_total[None]
    probability = jnp.exp(log_probability)
    grad = (weight_all * live)[None] * (
        row_advantage[None] * (probability - hit.astype(jnp.float32))
        + ENTROPY_WEIGHT * probability * (log_probability + entropy[None])
    )
    grad = lax.all_gather(grad.astype(jnp.bfloat16), "x", axis=0, tiled=True)
    contract = (((0,), (1,)), ((), ()))
    hidden_grad = lax.dot_general(
        grad[:vocab], head_weight, contract, preferred_element_type=jnp.float32
    ) + lax.dot_general(grad[vocab:], other_weight, contract, preferred_element_type=jnp.float32)
    hidden_grad = hidden_grad.astype(jnp.bfloat16).reshape(Y, per_tok, depth)
    hidden_grad = lax.all_to_all(hidden_grad, "y", 0, 0, tiled=True)
    hidden_grad = jnp.sum(hidden_grad.astype(jnp.float32), axis=0).astype(jnp.bfloat16)
    hidden_grad = lax.all_to_all(hidden_grad.reshape(Z, per_tok // Z, depth), "z", 0, 0, tiled=True)
    hidden_grad = jnp.sum(hidden_grad.astype(jnp.float32), axis=0)
    return hidden_grad.astype(jnp.bfloat16), loss


def solution(mesh):
    split = Mesh(mesh.devices.reshape(Y, C, Z, X), ("y", "c", "z", "x"))
    voc = ("y", "c", "z")
    return jax.shard_map(
        per_device,
        mesh=split,
        in_specs=(P(voc, "x"), P("x", voc), P(), P(), P(), P(), P()),
        out_specs=(P(voc, "x"), P()),
        check_vma=False,
    )
```

time: 1270 us -> 155 us (0.12)
  the two profiles are of different devices: /device:TPU:2 before, /device:TPU:32 now
where the time goes in v1:
time: 155 us; the launch traced here: 154 us
  blocking collectives  72.4 us (47%)
  waiting for transfers between devices  42.5 us (27%)
  starting transfers between devices  22.4 us (14%)
  matrix products  5.73 us (4%)
  other arithmetic  4.08 us (3%)
  between operations  3.83 us (2%)
  local copies, waits for them, and re-layouts  3.06 us (2%)
    all_to_all x1, blocking collectives, spread(): return lax.all_to_all(sent, axes, 0, 0, tiled=True)  32.7 us
    all_to_all x2, waiting for transfers between devices, spread(): return lax.all_to_all(sent, axes, 0, 0, tiled=True)  18 us
    all_gather x1, blocking collectives, per_device(): my_rows = lax.all_gather(tok_rows, 'y', axis=0, tiled=True)  14.3 us
    all_to_all x1, waiting for transfers between devices, per_device(): part = lax.all_to_all(part.reshape(X, chunk, rows), 'x', 0, 0, tiled=True)  13.4 us
    all_gather x1, blocking collectives, per_device(): grad = lax.all_gather(grad.astype(jnp.bfloat16), 'x', axis=0, tiled=True)  12.8 us
    all_to_all x1, blocking collectives, per_device(): hidden_grad = lax.all_to_all(hidden_grad, 'y', 0, 0, tiled=True)  12.6 us
    all_to_all x1, waiting for transfers between devices, per_device(): lax.all_to_all(hidden_grad.reshape(Z, per_tok // Z, depth), 'z', 0, 0, ti...  9.75 us
    all_to_all x2, starting transfers between devices, spread(): return lax.all_to_all(sent, axes, 0, 0, tiled=True)  9.42 us
  transfers between devices with their start and end apart: 6, of which 5 were waited for; matrix products, arithmetic and copies ran while one was open for 2% of the time, Pallas kernels for 0%

profile of v1, /device:TPU:32, one launch (start us, length us, event | category | flops | bytes accessed | tf_op | source)
XLA Modules:
  0.0 154.0 jit_solution(2962030888594878580)
XLA Ops:
  0.6 2.1 %collective-permute-start = (bf16[1792,512]{1,0:T(8,128)(2,1)}, bf16[1792,512]{1,0:T(8,128)(2,1)}, u32[]{:S(2)}, u32[]{:S(2)}) collective-permute-start(bf16[1792,512]{1,0:T(8,128)(2,1)} %param.8), channel_id=1, source_target_pairs={{0,64},{64,0},{1,65},{65,1},{2,66},{66,2},{3,67},{67,3},{4,68},{68... | collective-permute-start | bytes 5505032 | tf_op jit(solution)/shard_map/ppermute | solution.py:30
  2.7 0.8 broadcast_in_dim.9
  3.5 32.7 %all_to_all.30 = bf16[16,4,1792]{2,1,0:T(4,128)(2,1)S(1)} all-to-all(bf16[16,4,1792]{2,1,0:T(4,128)(2,1)S(1)} %broadcast_in_dim.9), channel_id=1, replica_groups=mesh['y'=4,'c'=2,'z'=16,'x'=4] {'z'}, dimensions={0} | all-to-all | bytes 458752 | tf_op jit(solution)/shard_map/all_to_all | solution.py:23
  36.3 14.3 %all_gather.6 = bf16[256,1792]{1,0:T(8,128)(2,1)S(1)} all-gather(bf16[64,1792]{1,0:T(8,128)(2,1)S(1)} %reshape.78), channel_id=1, replica_groups=mesh['y'=4,'c'=2,'z'=16,'x'=4] {'y'}, dimensions={0}, use_global_device_ids=true | all-gather | bytes 1146880 | tf_op jit(solution)/shard_map/all_gather | solution.py:49
  50.6 0.7 fusion.26
  51.3 2.2 %fusion.27 = f32[512,256]{1,0:T(8,128)S(1)} fusion(bf16[1792,512]{1,0:T(8,128)(2,1)} %collective-permute-done, bf16[256,1792]{1,0:T(8,128)(2,1)S(1)} %all_gather.6), kind=kOutput, calls=%fused_computation.65 | convolution fusion | flops 469762048 | bytes 3276800 | tf_op jit(solution)/shard_map/dot_general | solution.py:54
  53.5 1.1 pad_maximum_fusion
  54.6 4.4 %all-to-all-start.1 = ((f32[4,256,256]{2,1,0:T(8,128)}), f32[4,256,256]{2,1,0:T(8,128)S(1)}, u32[]{:S(2)}, u32[]{:S(2)}) async-start(f32[4,256,256]{2,1,0:T(8,128)} %bitcast), calls=%async_computation.1 | async-start | bytes 2097152 | tf_op jit(solution)/shard_map/all_to_all | solution.py:59
  59.0 0.1 select_reduce_fusion.2
  59.4 13.4 %all-to-all-done.1 = f32[4,256,256]{2,1,0:T(8,128)S(1)} async-done(((f32[4,256,256]{2,1,0:T(8,128)}), f32[4,256,256]{2,1,0:T(8,128)S(1)}, u32[]{:S(2)}, u32[]{:S(2)}) %all-to-all-start.1) | async-done | bytes 1048608 | tf_op jit(solution)/shard_map/all_to_all | solution.py:59
  72.9 0.1 exponential_reduce_fusion
  73.1 0.6 broadcast_in_dim.11
  73.7 5.8 %all-to-all-start.2 = ((f32[16,4,256]{2,1,0:T(4,128)}), f32[16,4,256]{2,1,0:T(4,128)S(1)}, u32[]{:S(2)}, u32[]{:S(2)}) async-start(f32[16,4,256]{2,1,0:T(4,128)} %broadcast_in_dim.11), calls=%async_computation.2 | async-start | bytes 131072 | tf_op jit(solution)/shard_map/all_to_all | solution.py:23
  79.5 0.6 fusion.25
  80.8 10.5 %all-to-all-done.2 = f32[16,4,256]{2,1,0:T(4,128)S(1)} async-done(((f32[16,4,256]{2,1,0:T(4,128)}), f32[16,4,256]{2,1,0:T(4,128)S(1)}, u32[]{:S(2)}, u32[]{:S(2)}) %all-to-all-start.2) | async-done | bytes 65568 | tf_op jit(solution)/shard_map/all_to_all | solution.py:23
  91.4 0.6 broadcast_in_dim.12
  92.1 3.6 %all-to-all-start.3 = ((f32[16,4,256]{2,1,0:T(4,128)}), f32[16,4,256]{2,1,0:T(4,128)S(1)}, u32[]{:S(2)}, u32[]{:S(2)}) async-start(f32[16,4,256]{2,1,0:T(4,128)} %broadcast_in_dim.12), calls=%async_computation.3 | async-start | bytes 131072 | tf_op jit(solution)/shard_map/all_to_all | solution.py:23
  95.7 0.1 convert_reduce_fusion
  95.8 7.6 %all-to-all-done.3 = f32[16,4,256]{2,1,0:T(4,128)S(1)} async-done(((f32[16,4,256]{2,1,0:T(4,128)}), f32[16,4,256]{2,1,0:T(4,128)S(1)}, u32[]{:S(2)}, u32[]{:S(2)}) %all-to-all-start.3) | async-done | bytes 65568 | tf_op jit(solution)/shard_map/all_to_all | solution.py:23
  103.4 0.6 multiply_reduce_fusion.2
  104.1 0.1 fusion.6
  104.2 12.8 %all_gather.7 = bf16[1024,256]{1,0:T(8,128)(2,1)S(1)} all-gather(bf16[256,256]{1,0:T(8,128)(2,1)S(1)} %fusion.6), channel_id=1, replica_groups=mesh['y'=4,'c'=2,'z'=16,'x'=4] {'x'}, dimensions={0}, use_global_device_ids=true | all-gather | bytes 655360 | tf_op jit(solution)/shard_map/all_gather | solution.py:87
  117.0 0.7 fusion.9
  117.7 2.2 %fusion = bf16[256,1792]{1,0:T(8,128)(2,1)S(1)} fusion(f32[256,1792]{1,0:T(8,128)S(1)} %fusion.9, bf16[1792,512]{1,0:T(8,128)(2,1)} %collective-permute-done, bf16[1024,256]{1,0:T(8,128)(2,1)S(1)} %all_gather.7), kind=kOutput, calls=%fused_computation.1 | convolution fusion | flops 470679552 | bytes 4849664 | tf_op jit(solution)/shard_map/dot_general | solution.py:91
  119.9 12.6 %all_to_all.31 = bf16[4,64,1792]{2,1,0:T(8,128)(2,1)S(1)} all-to-all(bf16[4,64,1792]{2,1,0:T(8,128)(2,1)S(1)} %bitcast.56), channel_id=1, replica_groups=mesh['y'=4,'c'=2,'z'=16,'x'=4] {'y'}, dimensions={0} | all-to-all | bytes 1835008 | tf_op jit(solution)/shard_map/all_to_all | solution.py:93
  132.5 0.2 reduce_sum.182
  132.6 0.7 reshape.82
  133.4 4.6 %all-to-all-start.5 = ((bf16[16,4,1792]{2,1,0:T(4,128)(2,1)}), bf16[16,4,1792]{2,1,0:T(4,128)(2,1)S(1)}, u32[]{:S(2)}, u32[]{:S(2)}) async-start(bf16[16,4,1792]{2,1,0:T(4,128)(2,1)} %reshape.82), calls=%async_computation.5 | async-start | bytes 458752 | tf_op jit(solution)/shard_map/all_to_all | solution.py:95
  137.9 1.9 %collective-permute-start.1 = (f32[]{:T(128)}, f32[]{:T(128)}, u32[]{:S(2)}, u32[]{:S(2)}) collective-permute-start(f32[]{:T(128)} %get-tuple-element.15), channel_id=1, source_target_pairs={{0,64},{64,0},{1,65},{65,1},{2,66},{66,2},{3,67},{67,3},{4,68},{68... | collective-permute-start | bytes 20 | tf_op jit(solution)/shard_map/ppermute | solution.py:79
  139.9 1.4 collective-permute-done.1
  142.4 9.8 %all-to-all-done.5 = bf16[16,4,1792]{2,1,0:T(4,128)(2,1)S(1)} async-done(((bf16[16,4,1792]{2,1,0:T(4,128)(2,1)}), bf16[16,4,1792]{2,1,0:T(4,128)(2,1)S(1)}, u32[]{:S(2)}, u32[]{:S(2)}) %all-to-all-start.5) | async-done | bytes 229408 | tf_op jit(solution)/shard_map/all_to_all | solution.py:95
  152.2 0.7 reduce_sum.183
  (30 shorter events, 0.7 us)
Async XLA Ops:
  0.6 49.9 %copy-start = (bf16[1792,512]{1,0:T(8,128)(2,1)S(1)}, bf16[1792,512]{1,0:T(8,128)(2,1)}, u32[]{:S(2)}) copy-start(bf16[1792,512]{1,0:T(8,128)(2,1)} %param.8) | copy-start | bytes 5505028
  0.6 50.6 %collective-permute-start = (bf16[1792,512]{1,0:T(8,128)(2,1)}, bf16[1792,512]{1,0:T(8,128)(2,1)}, u32[]{:S(2)}, u32[]{:S(2)}) collective-permute-start(bf16[1792,512]{1,0:T(8,128)(2,1)} %param.8), channel_id=1, source_target_pairs={{0,64},{64,0},{1,65},{65,1},{2,66},{66,2},{3,67},{67,3},{4,68},{68... | collective-permute-start | bytes 5505032 | tf_op jit(solution)/shard_map/ppermute | solution.py:30
  53.5 5.5 %copy-start.4 = (s32[32]{0:T(128)S(1)}, s32[32]{0:T(128)}, u32[]{:S(2)}) copy-start(s32[32]{0:T(128)} %param.12) | copy-start | bytes 388
  53.5 5.5 %copy-start.5 = (f32[32]{0:T(128)S(1)}, f32[32]{0:T(128)}, u32[]{:S(2)}) copy-start(f32[32]{0:T(128)} %param.13) | copy-start | bytes 388
  53.5 5.7 %copy-start.1 = (s32[512]{0:T(512)S(1)}, s32[512]{0:T(512)}, u32[]{:S(2)}) copy-start(s32[512]{0:T(512)} %param.9) | copy-start | bytes 6148
  54.6 24.9 %copy-start.2 = (s32[32]{0:T(128)S(1)}, s32[32]{0:T(128)}, u32[]{:S(2)}) copy-start(s32[32]{0:T(128)} %param.10) | copy-start | bytes 388
  54.6 24.9 %copy-start.3 = (s32[32]{0:T(128)S(1)}, s32[32]{0:T(128)}, u32[]{:S(2)}) copy-start(s32[32]{0:T(128)} %param.11) | copy-start | bytes 388
  54.6 18.2 %all-to-all-start.1 = ((f32[4,256,256]{2,1,0:T(8,128)}), f32[4,256,256]{2,1,0:T(8,128)S(1)}, u32[]{:S(2)}, u32[]{:S(2)}) async-start(f32[4,256,256]{2,1,0:T(8,128)} %bitcast), calls=%async_computation.1 | async-start | bytes 2097152 | tf_op jit(solution)/shard_map/all_to_all | solution.py:59
  73.7 17.6 %all-to-all-start.2 = ((f32[16,4,256]{2,1,0:T(4,128)}), f32[16,4,256]{2,1,0:T(4,128)S(1)}, u32[]{:S(2)}, u32[]{:S(2)}) async-start(f32[16,4,256]{2,1,0:T(4,128)} %broadcast_in_dim.11), calls=%async_computation.2 | async-start | bytes 131072 | tf_op jit(solution)/shard_map/all_to_all | solution.py:23
  92.1 11.3 %all-to-all-start.3 = ((f32[16,4,256]{2,1,0:T(4,128)}), f32[16,4,256]{2,1,0:T(4,128)S(1)}, u32[]{:S(2)}, u32[]{:S(2)}) async-start(f32[16,4,256]{2,1,0:T(4,128)} %broadcast_in_dim.12), calls=%async_computation.3 | async-start | bytes 131072 | tf_op jit(solution)/shard_map/all_to_all | solution.py:23
  133.4 18.8 %all-to-all-start.5 = ((bf16[16,4,1792]{2,1,0:T(4,128)(2,1)}), bf16[16,4,1792]{2,1,0:T(4,128)(2,1)S(1)}, u32[]{:S(2)}, u32[]{:S(2)}) async-start(bf16[16,4,1792]{2,1,0:T(4,128)(2,1)} %reshape.82), calls=%async_computation.5 | async-start | bytes 458752 | tf_op jit(solution)/shard_map/all_to_all | solution.py:95
  137.9 3.3 %collective-permute-start.1 = (f32[]{:T(128)}, f32[]{:T(128)}, u32[]{:S(2)}, u32[]{:S(2)}) collective-permute-start(f32[]{:T(128)} %get-tuple-element.15), channel_id=1, source_target_pairs={{0,64},{64,0},{1,65},{65,1},{2,66},{66,2},{3,67},{67,3},{4,68},{68... | collective-permute-start | bytes 20 | tf_op jit(solution)/shard_map/ppermute | solution.py:79

commit v2 on v1

v2 whole, which is shorter than its diff:
```python
import jax
import jax.numpy as jnp
from jax import lax
from jax.experimental import pallas as pl
from jax.experimental.pallas import tpu as pltpu
from jax.sharding import Mesh, PartitionSpec as P

GROUP_SIZE = 16
GROUPS = 2
ENTROPY_WEIGHT = 0.2
Y, C, Z, X = 4, 2, 16, 4
VMEM = pl.BlockSpec(memory_space=pltpu.VMEM)
ANY = pl.BlockSpec(memory_space=pl.ANY)
PARAMS = pltpu.CompilerParams(vmem_limit_bytes=24 * 1024 * 1024)


def combine(stats):
    top = jnp.max(stats[:, 0], axis=0)
    scale = jnp.exp(stats[:, 0] - top[None])
    total = jnp.sum(scale * stats[:, 1], axis=0)
    weighted = jnp.sum(scale * (stats[:, 2] + (stats[:, 0] - top[None]) * stats[:, 1]), axis=0)
    target = jnp.sum(stats[:, 3], axis=0)
    return jnp.stack([top, total, weighted, target])


def spread(block, axes, n):
    sent = jnp.broadcast_to(block[None], (n, *block.shape))
    return lax.all_to_all(sent, axes, 0, 0, tiled=True)


def first_column(chunk, vocab, width):
    y, c, z = (lax.axis_index(a) for a in ("y", "c", "z"))
    per_core = vocab // width
    other = chunk // per_core
    core = c + other * (1 - 2 * c)
    return ((2 * y + core) * Z + z) * vocab + (chunk % per_core) * width


def logits_kernel(rows_ref, own_ref, other_hbm, out_ref, other_ref, sem):
    fetch = pltpu.make_async_copy(other_hbm, other_ref, sem)
    fetch.start()
    width = out_ref.shape[2]
    per_core = X // C
    for k in range(X):
        if k == per_core:
            fetch.wait()
        w_ref = own_ref if k < per_core else other_ref
        at = k % per_core * width
        out_ref[k] = jnp.dot(
            rows_ref[...], w_ref[:, at : at + width], preferred_element_type=jnp.float32
        )


def partial_logits(rows, own, other):
    n, depth = rows.shape
    vocab = own.shape[1]
    width = C * vocab // X
    return pl.pallas_call(
        logits_kernel,
        out_shape=jax.ShapeDtypeStruct((X, n, width), jnp.float32),
        in_specs=[VMEM, VMEM, ANY],
        out_specs=VMEM,
        scratch_shapes=[pltpu.VMEM(other.shape, other.dtype), pltpu.SemaphoreType.DMA],
        compiler_params=PARAMS,
        cost_estimate=pl.CostEstimate(
            flops=2 * n * depth * C * vocab, bytes_accessed=4 * X * n * width, transcendentals=0
        ),
        name="partial_logits",
    )(rows, own, other)


def stats_kernel(vocab, part_ref, target_ref, logits_ref, stats_ref):
    logits = part_ref[0] + part_ref[1] + part_ref[2] + part_ref[3]
    logits_ref[...] = logits
    n, width = logits.shape
    top = jnp.max(logits, axis=1, keepdims=True)
    shifted = logits - top
    e = jnp.exp(shifted)
    column = lax.broadcasted_iota(jnp.int32, (n, width), 1) + first_column(lax.axis_index("x"), vocab, width)
    hit = column == target_ref[...]
    values = (
        top,
        jnp.sum(e, axis=1, keepdims=True),
        jnp.sum(e * shifted, axis=1, keepdims=True),
        jnp.sum(jnp.where(hit, logits, 0.0), axis=1, keepdims=True),
    )
    lane = lax.broadcasted_iota(jnp.int32, (n, 128), 1)
    packed = jnp.zeros((n, 128), jnp.float32)
    for i, value in enumerate(values):
        packed = jnp.where(lane == i, value, packed)
    packed = packed.T[:8]
    for i in range(Z):
        stats_ref[i] = packed


def local_stats(part, target, vocab):
    _, n, width = part.shape
    return pl.pallas_call(
        lambda *refs: stats_kernel(vocab, *refs),
        out_shape=(
            jax.ShapeDtypeStruct((n, width), jnp.float32),
            jax.ShapeDtypeStruct((Z, 8, n), jnp.float32),
        ),
        in_specs=[VMEM, VMEM],
        out_specs=(VMEM, VMEM),
        compiler_params=PARAMS,
        cost_estimate=pl.CostEstimate(
            flops=8 * n * width, bytes_accessed=4 * X * n * width, transcendentals=n * width
        ),
        name="local_stats",
    )(part, target)


def grad_kernel(
    vocab, stats_ref, meta_ref, target_ref, l0, l1, l2, l3, own_ref, other_hbm, out_ref, loss_ref,
    g_ref, other_ref, sem
):
    fetch = pltpu.make_async_copy(other_hbm, other_ref, sem)
    fetch.start()
    tops = stats_ref[:, 0]
    top = jnp.max(tops, axis=0, keepdims=True)
    gap = tops - top
    scale = jnp.exp(gap)
    total = jnp.sum(scale * stats_ref[:, 1], axis=0, keepdims=True)
    weighted = jnp.sum(scale * (stats_ref[:, 2] + gap * stats_ref[:, 1]), axis=0, keepdims=True)
    target_value = jnp.sum(stats_ref[:, 3], axis=0, keepdims=True)
    log_sum = jnp.log(total)
    log_total = top + log_sum
    entropy = log_sum - weighted / total
    live, advantage, weight = meta_ref[0:1], meta_ref[1:2], meta_ref[2:3]
    row_loss = live * (-advantage * (target_value - log_total) - ENTROPY_WEIGHT * entropy)
    loss_ref[...] = jnp.sum(row_loss, axis=1, keepdims=True)

    n = live.shape[1]
    row = lax.broadcasted_iota(jnp.int32, (128, n), 0)
    packed = jnp.zeros((128, n), jnp.float32)
    for i, value in enumerate((log_total, entropy, weight * live, advantage)):
        packed = jnp.where(row == i, value, packed)
    packed = packed.T
    log_total, entropy, row_weight, advantage = (packed[:, i : i + 1] for i in range(4))
    width = l0.shape[1]
    x = lax.axis_index("x")
    target = target_ref[...]
    for k, l_ref in enumerate((l0, l1, l2, l3)):
        chunk = lax.rem(x + k, X)
        log_probability = l_ref[...] - log_total
        probability = jnp.exp(log_probability)
        column = lax.broadcasted_iota(jnp.int32, (n, width), 1) + first_column(chunk, vocab, width)
        hit = jnp.where(column == target, 1.0, 0.0)
        grad = row_weight * (
            advantage * (probability - hit)
            + ENTROPY_WEIGHT * probability * (log_probability + entropy)
        )
        g_ref[:, pl.ds(pl.multiple_of(chunk * width, width), width)] = grad.astype(jnp.bfloat16)
    contract = (((1,), (1,)), ((), ()))
    depth = own_ref.shape[0]
    step = 256
    fetch.wait()
    for at in range(0, depth, step):
        part = lax.dot_general(
            g_ref[:, :vocab], own_ref[at : at + step], contract, preferred_element_type=jnp.float32
        ) + lax.dot_general(
            g_ref[:, vocab:], other_ref[at : at + step], contract, preferred_element_type=jnp.float32
        )
        out_ref[:, at : at + step] = part.astype(jnp.bfloat16)


def partial_grad(stats, meta, target, chunks, own, other):
    n, width = chunks[0].shape
    depth, vocab = own.shape
    return pl.pallas_call(
        lambda *refs: grad_kernel(vocab, *refs),
        out_shape=(
            jax.ShapeDtypeStruct((n, depth), jnp.bfloat16),
            jax.ShapeDtypeStruct((1, 1), jnp.float32),
        ),
        in_specs=[VMEM] * 8 + [ANY],
        out_specs=(VMEM, VMEM),
        scratch_shapes=[
            pltpu.VMEM((n, C * vocab), jnp.bfloat16),
            pltpu.VMEM(other.shape, other.dtype),
            pltpu.SemaphoreType.DMA,
        ],
        compiler_params=PARAMS,
        cost_estimate=pl.CostEstimate(
            flops=2 * n * depth * C * vocab,
            bytes_accessed=4 * X * n * width,
            transcendentals=X * n * width,
        ),
        name="partial_grad",
    )(stats, meta, target, *chunks, own, other)


def per_device(hidden, head_weight, targets, offsets, lengths, group_ids, rewards):
    c = lax.axis_index("c")
    depth, vocab = head_weight.shape
    total_rows = targets.shape[0]

    rows = total_rows // C
    place = jnp.arange(rows, dtype=jnp.int32)
    per_tok = total_rows // (Y * C)
    row_index = (2 * (place // per_tok) + c) * per_tok + place % per_tok
    member = (
        (row_index[None, :] >= offsets[:, None])
        & (row_index[None, :] < (offsets + lengths)[:, None])
    ).astype(jnp.float32)
    live = jnp.sum(member, axis=0)
    grouping = (group_ids[:, None] == jnp.arange(GROUPS, dtype=jnp.int32)[None, :]).astype(jnp.float32)
    group_mean = jnp.sum(rewards[:, None] * grouping, axis=0) / GROUP_SIZE
    advantage = rewards - jnp.sum(grouping * group_mean[None, :], axis=1)
    row_advantage = jnp.sum(member * advantage[:, None], axis=0)
    weight_all = total_rows / jnp.sum(lengths).astype(jnp.float32)
    meta = jnp.stack([live, row_advantage, jnp.broadcast_to(weight_all, (rows,))])
    own_targets = targets.reshape(Y, C, per_tok)[:, c].reshape(rows, 1)

    swap = [(0, 1), (1, 0)]
    tok_rows = spread(hidden, "z", Z).reshape(per_tok, depth)
    other_weight = lax.ppermute(head_weight, "c", swap)
    tok_rows, meta, own_targets = lax.optimization_barrier((tok_rows, meta, own_targets))
    my_rows = lax.all_gather(tok_rows, "y", axis=0, tiled=True)

    part = partial_logits(my_rows, head_weight, other_weight)
    part = lax.all_to_all(part, "x", 0, 0, tiled=True)
    logits, stats = local_stats(part, own_targets, vocab)
    stats = lax.all_to_all(stats, "z", 0, 0, tiled=True)
    chunks = [logits] + [
        lax.ppermute(logits, "x", [((i + k) % X, i) for i in range(X)]) for k in range(1, X)
    ]
    stats = combine(stats[:, :4])
    stats = spread(stats, ("y", "x"), Y * X)
    hidden_grad, loss = partial_grad(stats, meta, own_targets, chunks, head_weight, other_weight)
    loss = loss[0, 0]

    hidden_grad = lax.all_to_all(hidden_grad.reshape(Y, per_tok, depth), "y", 0, 0, tiled=True)
    hidden_grad = jnp.sum(hidden_grad.astype(jnp.float32), axis=0).astype(jnp.bfloat16)
    hidden_grad = lax.all_to_all(hidden_grad.reshape(Z, per_tok // Z, depth), "z", 0, 0, tiled=True)
    hidden_grad = jnp.sum(hidden_grad.astype(jnp.float32), axis=0)
    loss = weight_all * (loss + lax.ppermute(loss, "c", swap))
    return hidden_grad.astype(jnp.bfloat16), loss


def solution(mesh):
    split = Mesh(mesh.devices.reshape(Y, C, Z, X), ("y", "c", "z", "x"))
    voc = ("y", "c", "z")
    return jax.shard_map(
        per_device,
        mesh=split,
        in_specs=(P(voc, "x"), P("x", voc), P(), P(), P(), P(), P()),
        out_specs=(P(voc, "x"), P()),
        check_vma=False,
    )
```

time: 155 us -> 148 us (0.955)
  blocking collectives: 72.4 us -> 26.9 us
  starting transfers between devices: 22.4 us -> 51.3 us
  Pallas kernels: 0 us -> 6.28 us
  waiting for transfers between devices: 42.5 us -> 48.5 us
  matrix products: 5.73 us -> 0 us
  local copies, waits for them, and re-layouts: 3.06 us -> 4.96 us
    all_to_all x2 -> x1, blocking collectives: 45.4 us -> 12.6 us  [per_device(): lax.all_to_all(hidden_grad.reshape(Y, per_tok, depth), 'y', 0, 0, tiled=T...]
    all_gather x1 -> x0, blocking collectives: 12.8 us -> none  [per_device(): grad = lax.all_gather(grad.astype(jnp.bfloat16), 'x', axis=0, tiled=True)]
    all_to_all x2, starting transfers between devices: 9.42 us -> 18.8 us  [spread(): return lax.all_to_all(sent, axes, 0, 0, tiled=True)]
    ppermute x2 -> x5, starting transfers between devices: 3.96 us -> 12.3 us  [the longest x3 8.36 us: per_device(): lax.ppermute(logits, 'x', [((i + k) % X, i) for i in range(X)])]
    pallas_call x0 -> x3, Pallas kernels: none -> 6.28 us  [the longest x1 3.13 us: partial_grad(): pl.pallas_call(lambda *refs: grad_kernel(vocab, *refs), out_shape=(jax.Sh...]
    dot_general x4 -> x0, matrix products: 5.73 us -> none  [the longest x2 2.86 us: per_device(): lax.dot_general(w, my_rows, contract, preferred_element_type=jnp.float32)]
    all_to_all x1 -> x2, starting transfers between devices: 4.43 us -> 10.1 us  [the longest x1 5.81 us: per_device(): stats = lax.all_to_all(stats, 'z', 0, 0, tiled=True)]
    all_to_all x1, starting transfers between devices: 4.58 us -> 10.1 us  [per_device(): lax.all_to_all(hidden_grad.reshape(Z, per_tok // Z, depth), 'z', 0, 0, ti...]
  transfers between devices with their start and end apart: 6 -> 10, of which waited for: 5 -> 7; matrix products, arithmetic and copies ran while one was open for 2% -> 5% of each run, Pallas kernels for 0% -> 0%
where the time goes in v2:
time: 148 us; the launch traced here: 147 us
  starting transfers between devices  51.3 us (35%)
  waiting for transfers between devices  48.5 us (33%)
  blocking collectives  26.9 us (18%)
  Pallas kernels  6.28 us (4%)
  other arithmetic  5.29 us (4%)
  local copies, waits for them, and re-layouts  4.96 us (3%)
  between operations  3.81 us (3%)
    all_to_all x2, waiting for transfers between devices, spread(): return lax.all_to_all(sent, axes, 0, 0, tiled=True)  19.1 us
    all_to_all x2, starting transfers between devices, spread(): return lax.all_to_all(sent, axes, 0, 0, tiled=True)  18.8 us
    all_gather x1, blocking collectives, per_device(): my_rows = lax.all_gather(tok_rows, 'y', axis=0, tiled=True)  14.3 us
    all_to_all x1, waiting for transfers between devices, per_device(): part = lax.all_to_all(part, 'x', 0, 0, tiled=True)  13.7 us
    all_to_all x1, blocking collectives, per_device(): lax.all_to_all(hidden_grad.reshape(Y, per_tok, depth), 'y', 0, 0, tiled=T...  12.6 us
    all_to_all x1, starting transfers between devices, per_device(): lax.all_to_all(hidden_grad.reshape(Z, per_tok // Z, depth), 'z', 0, 0, ti...  10.1 us
    all_to_all x1, waiting for transfers between devices, per_device(): lax.all_to_all(hidden_grad.reshape(Z, per_tok // Z, depth), 'z', 0, 0, ti...  9.71 us
    ppermute x3, starting transfers between devices, per_device(): lax.ppermute(logits, 'x', [((i + k) % X, i) for i in range(X)])  8.36 us
  transfers between devices with their start and end apart: 10, of which 7 were waited for; matrix products, arithmetic and copies ran while one was open for 5% of the time, Pallas kernels for 0%

profile of v2, /device:TPU:32, one launch (start us, length us, event | category | flops | bytes accessed | tf_op | source)
XLA Modules:
  0.0 147.0 jit_solution(13305536273877710666)
XLA Ops:
  0.6 2.1 %collective-permute-start = (bf16[1792,512]{1,0:T(8,128)(2,1)}, bf16[1792,512]{1,0:T(8,128)(2,1)}, u32[]{:S(2)}, u32[]{:S(2)}) collective-permute-start(bf16[1792,512]{1,0:T(8,128)(2,1)} %refs_7_.1), channel_id=1, source_target_pairs={{0,64},{64,0},{1,65},{65,1},{2,66},{66,2},{3,67},{67,3},{4,68},{68... | collective-permute-start | bytes 5505032 | tf_op jit(solution)/shard_map/ppermute | solution.py:218
  2.7 1.5 broadcast_in_dim.4
  4.2 15.2 %all-to-all-start = ((bf16[16,4,1792]{2,1,0:T(4,128)(2,1)}), bf16[16,4,1792]{2,1,0:T(4,128)(2,1)S(1)}, u32[]{:S(2)}, u32[]{:S(2)}) async-start(bf16[16,4,1792]{2,1,0:T(4,128)(2,1)} %broadcast_in_dim.4), calls=%async_computation | async-start | bytes 458752 | tf_op jit(solution)/shard_map/all_to_all | solution.py:28
  19.4 0.8 select_reduce_fusion.2
  20.2 0.7 select_reduce_fusion.1
  20.9 0.7 sub.22
  21.6 1.3 fusion.10
  23.5 0.8 reshape.52
  24.5 0.7 convert_reduce_fusion
  25.4 11.8 %all-to-all-done = bf16[16,4,1792]{2,1,0:T(4,128)(2,1)S(1)} async-done(((bf16[16,4,1792]{2,1,0:T(4,128)(2,1)}), bf16[16,4,1792]{2,1,0:T(4,128)(2,1)S(1)}, u32[]{:S(2)}, u32[]{:S(2)}) %all-to-all-start) | async-done | bytes 229408 | tf_op jit(solution)/shard_map/all_to_all | solution.py:28
  37.2 14.3 %all_gather.3.rows_ref = bf16[256,1792]{1,0:T(8,128)(2,1)S(1)} all-gather(bf16[64,1792]{1,0:T(8,128)(2,1)S(1)} %reshape.51), channel_id=1, replica_groups=mesh['y'=4,'c'=2,'z'=16,'x'=4] {'y'}, dimensions={0}, use_global_device_ids=true | all-gather | bytes 1146880 | tf_op jit(solution)/shard_map/all_gather | solution.py:220
  51.5 2.2 %partial_logits.1 = f32[4,256,256]{2,1,0:T(8,128)S(1)} custom-call(bf16[256,1792]{1,0:T(8,128)(2,1)S(1)} %all_gather.3.rows_ref, bf16[1792,512]{1,0:T(8,128)(2,1)S(1)} %copy-done, bf16[1792,512]{1,0:T(8,128)(2,1)} %collective-permute-done.other_hbm.refs_8_), custom_call_target="tpu_custom_call" | custom-call | flops 939524096 | bytes 1048576 | tf_op jit(solution)/shard_map/partial_logits/pallas_call | solution.py:58
  53.6 1.0 copy-done.1
  54.6 4.3 %all-to-all-start.1 = ((f32[4,256,256]{2,1,0:T(8,128)}), f32[4,256,256]{2,1,0:T(8,128)S(1)}, u32[]{:S(2)}, u32[]{:S(2)}) async-start(f32[4,256,256]{2,1,0:T(8,128)} %copy-done.1), calls=%async_computation.1 | async-start | bytes 2097152 | tf_op jit(solution)/shard_map/all_to_all | solution.py:223
  59.1 13.7 %all-to-all-done.1.refs_0_ = f32[4,256,256]{2,1,0:T(8,128)S(1)} async-done(((f32[4,256,256]{2,1,0:T(8,128)}), f32[4,256,256]{2,1,0:T(8,128)S(1)}, u32[]{:S(2)}, u32[]{:S(2)}) %all-to-all-start.1) | async-done | bytes 1048608 | tf_op jit(solution)/shard_map/all_to_all | solution.py:223
  72.7 1.0 local_stats.1
  73.7 5.8 %all-to-all-start.2 = ((f32[16,8,256]{2,1,0:T(8,128)}), f32[16,8,256]{2,1,0:T(8,128)S(1)}, u32[]{:S(2)}, u32[]{:S(2)}) async-start(f32[16,8,256]{2,1,0:T(8,128)} %get-tuple-element.11), calls=%async_computation.2 | async-start | bytes 262144 | tf_op jit(solution)/shard_map/all_to_all | solution.py:225
  79.5 3.1 %collective-permute-start.1 = (f32[256,256]{1,0:T(8,128)S(1)}, f32[256,256]{1,0:T(8,128)S(1)}, u32[]{:S(2)}, u32[]{:S(2)}) collective-permute-start(f32[256,256]{1,0:T(8,128)S(1)} %get-tuple-element.13.refs_3_), channel_id=1, source_target_pairs={{1,0},{2,1},{3,2},{0,3},{5,4},{6,5},{7,6},{4,7},{9,8},{10,9},{11,1... | collective-permute-start | bytes 786440 | tf_op jit(solution)/shard_map/ppermute | solution.py:227
  82.6 3.4 %collective-permute-start.2 = (f32[256,256]{1,0:T(8,128)S(1)}, f32[256,256]{1,0:T(8,128)S(1)}, u32[]{:S(2)}, u32[]{:S(2)}) collective-permute-start(f32[256,256]{1,0:T(8,128)S(1)} %get-tuple-element.13.refs_3_), channel_id=1, source_target_pairs={{2,0},{3,1},{0,2},{1,3},{6,4},{7,5},{4,6},{5,7},{10,8},{11,9},{8,1... | collective-permute-start | bytes 786440 | tf_op jit(solution)/shard_map/ppermute | solution.py:227
  86.0 1.9 %collective-permute-start.3 = (f32[256,256]{1,0:T(8,128)S(1)}, f32[256,256]{1,0:T(8,128)S(1)}, u32[]{:S(2)}, u32[]{:S(2)}) collective-permute-start(f32[256,256]{1,0:T(8,128)S(1)} %get-tuple-element.13.refs_3_), channel_id=1, source_target_pairs={{3,0},{0,1},{1,2},{2,3},{7,4},{4,5},{5,6},{6,7},{11,8},{8,9},{9,10... | collective-permute-start | bytes 786440 | tf_op jit(solution)/shard_map/ppermute | solution.py:227
  87.9 4.3 %all-to-all-done.2 = f32[16,8,256]{2,1,0:T(8,128)S(1)} async-done(((f32[16,8,256]{2,1,0:T(8,128)}), f32[16,8,256]{2,1,0:T(8,128)S(1)}, u32[]{:S(2)}, u32[]{:S(2)}) %all-to-all-start.2) | async-done | bytes 131104 | tf_op jit(solution)/shard_map/all_to_all | solution.py:225
  92.4 0.6 broadcast_in_dim.5
  93.0 3.6 %all-to-all-start.3 = ((f32[16,4,256]{2,1,0:T(4,128)}), f32[16,4,256]{2,1,0:T(4,128)S(1)}, u32[]{:S(2)}, u32[]{:S(2)}) async-start(f32[16,4,256]{2,1,0:T(4,128)} %broadcast_in_dim.5), calls=%async_computation.3 | async-start | bytes 131072 | tf_op jit(solution)/shard_map/all_to_all | solution.py:28
  96.9 7.3 %all-to-all-done.3.refs_0_ = f32[16,4,256]{2,1,0:T(4,128)S(1)} async-done(((f32[16,4,256]{2,1,0:T(4,128)}), f32[16,4,256]{2,1,0:T(4,128)S(1)}, u32[]{:S(2)}, u32[]{:S(2)}) %all-to-all-start.3) | async-done | bytes 65568 | tf_op jit(solution)/shard_map/all_to_all | solution.py:28
  104.3 3.1 %partial_grad.1 = (bf16[256,1792]{1,0:T(8,128)(2,1)S(1)}, f32[1,1]{1,0:T(1,128)}) custom-call(f32[16,4,256]{2,1,0:T(4,128)S(1)} %all-to-all-done.3.refs_0_, f32[3,256]{1,0:T(4,128)S(1)} %maximum_maximum_fusion.refs_1_, s32[256,1]{1,0:T(8,128)S(1)} %copy.19.refs_1_.refs_2_, f32[256,256]{1,0:T(8,128)S(1)} %get-tuple-element.13.refs_3_, ...), custom_call_target="tpu_custom_call" | custom-call | flops 939524096 | bytes 1048576 | tf_op jit(solution)/shard_map/partial_grad/pallas_call | solution.py:171
  107.4 12.6 %all_to_all.30 = bf16[4,64,1792]{2,1,0:T(8,128)(2,1)S(1)} all-to-all(bf16[4,64,1792]{2,1,0:T(8,128)(2,1)S(1)} %bitcast.29), channel_id=1, replica_groups=mesh['y'=4,'c'=2,'z'=16,'x'=4] {'y'}, dimensions={0} | all-to-all | bytes 1835008 | tf_op jit(solution)/shard_map/all_to_all | solution.py:234
  120.2 0.7 reshape.54
  120.9 10.1 %all-to-all-start.5 = ((bf16[16,4,1792]{2,1,0:T(4,128)(2,1)}), bf16[16,4,1792]{2,1,0:T(4,128)(2,1)S(1)}, u32[]{:S(2)}, u32[]{:S(2)}) async-start(bf16[16,4,1792]{2,1,0:T(4,128)(2,1)} %reshape.54), calls=%async_computation.5 | async-start | bytes 458752 | tf_op jit(solution)/shard_map/all_to_all | solution.py:236
  131.0 1.9 %collective-permute-start.4 = (f32[]{:T(128)}, f32[]{:T(128)}, u32[]{:S(2)}, u32[]{:S(2)}) collective-permute-start(f32[]{:T(128)} %bitcast.9), channel_id=1, source_target_pairs={{0,64},{64,0},{1,65},{65,1},{2,66},{66,2},{3,67},{67,3},{4,68},{68... | collective-permute-start | bytes 20 | tf_op jit(solution)/shard_map/ppermute | solution.py:238
  132.9 1.4 collective-permute-done.4
  135.5 9.7 %all-to-all-done.5 = bf16[16,4,1792]{2,1,0:T(4,128)(2,1)S(1)} async-done(((bf16[16,4,1792]{2,1,0:T(4,128)(2,1)}), bf16[16,4,1792]{2,1,0:T(4,128)(2,1)S(1)}, u32[]{:S(2)}, u32[]{:S(2)}) %all-to-all-start.5) | async-done | bytes 229408 | tf_op jit(solution)/shard_map/all_to_all | solution.py:236
  145.2 0.7 reduce_sum.105
  (19 shorter events, 1.0 us)
Async XLA Ops:
  0.6 50.8 %copy-start = (bf16[1792,512]{1,0:T(8,128)(2,1)S(1)}, bf16[1792,512]{1,0:T(8,128)(2,1)}, u32[]{:S(2)}) copy-start(bf16[1792,512]{1,0:T(8,128)(2,1)} %refs_7_.1) | copy-start | bytes 5505028
  0.6 50.8 %collective-permute-start = (bf16[1792,512]{1,0:T(8,128)(2,1)}, bf16[1792,512]{1,0:T(8,128)(2,1)}, u32[]{:S(2)}, u32[]{:S(2)}) collective-permute-start(bf16[1792,512]{1,0:T(8,128)(2,1)} %refs_7_.1), channel_id=1, source_target_pairs={{0,64},{64,0},{1,65},{65,1},{2,66},{66,2},{3,67},{67,3},{4,68},{68... | collective-permute-start | bytes 5505032 | tf_op jit(solution)/shard_map/ppermute | solution.py:218
  4.2 32.9 %all-to-all-start = ((bf16[16,4,1792]{2,1,0:T(4,128)(2,1)}), bf16[16,4,1792]{2,1,0:T(4,128)(2,1)S(1)}, u32[]{:S(2)}, u32[]{:S(2)}) async-start(bf16[16,4,1792]{2,1,0:T(4,128)(2,1)} %broadcast_in_dim.4), calls=%async_computation | async-start | bytes 458752 | tf_op jit(solution)/shard_map/all_to_all | solution.py:28
  53.6 1.0 copy-start.1
  54.6 18.1 %all-to-all-start.1 = ((f32[4,256,256]{2,1,0:T(8,128)}), f32[4,256,256]{2,1,0:T(8,128)S(1)}, u32[]{:S(2)}, u32[]{:S(2)}) async-start(f32[4,256,256]{2,1,0:T(8,128)} %copy-done.1), calls=%async_computation.1 | async-start | bytes 2097152 | tf_op jit(solution)/shard_map/all_to_all | solution.py:223
  73.7 18.5 %all-to-all-start.2 = ((f32[16,8,256]{2,1,0:T(8,128)}), f32[16,8,256]{2,1,0:T(8,128)S(1)}, u32[]{:S(2)}, u32[]{:S(2)}) async-start(f32[16,8,256]{2,1,0:T(8,128)} %get-tuple-element.11), calls=%async_computation.2 | async-start | bytes 262144 | tf_op jit(solution)/shard_map/all_to_all | solution.py:225
  79.5 17.1 %collective-permute-start.1 = (f32[256,256]{1,0:T(8,128)S(1)}, f32[256,256]{1,0:T(8,128)S(1)}, u32[]{:S(2)}, u32[]{:S(2)}) collective-permute-start(f32[256,256]{1,0:T(8,128)S(1)} %get-tuple-element.13.refs_3_), channel_id=1, source_target_pairs={{1,0},{2,1},{3,2},{0,3},{5,4},{6,5},{7,6},{4,7},{9,8},{10,9},{11,1... | collective-permute-start | bytes 786440 | tf_op jit(solution)/shard_map/ppermute | solution.py:227
  82.6 14.0 %collective-permute-start.2 = (f32[256,256]{1,0:T(8,128)S(1)}, f32[256,256]{1,0:T(8,128)S(1)}, u32[]{:S(2)}, u32[]{:S(2)}) collective-permute-start(f32[256,256]{1,0:T(8,128)S(1)} %get-tuple-element.13.refs_3_), channel_id=1, source_target_pairs={{2,0},{3,1},{0,2},{1,3},{6,4},{7,5},{4,6},{5,7},{10,8},{11,9},{8,1... | collective-permute-start | bytes 786440 | tf_op jit(solution)/shard_map/ppermute | solution.py:227
  86.0 11.0 %collective-permute-start.3 = (f32[256,256]{1,0:T(8,128)S(1)}, f32[256,256]{1,0:T(8,128)S(1)}, u32[]{:S(2)}, u32[]{:S(2)}) collective-permute-start(f32[256,256]{1,0:T(8,128)S(1)} %get-tuple-element.13.refs_3_), channel_id=1, source_target_pairs={{3,0},{0,1},{1,2},{2,3},{7,4},{4,5},{5,6},{6,7},{11,8},{8,9},{9,10... | collective-permute-start | bytes 786440 | tf_op jit(solution)/shard_map/ppermute | solution.py:227
  93.0 11.3 %all-to-all-start.3 = ((f32[16,4,256]{2,1,0:T(4,128)}), f32[16,4,256]{2,1,0:T(4,128)S(1)}, u32[]{:S(2)}, u32[]{:S(2)}) async-start(f32[16,4,256]{2,1,0:T(4,128)} %broadcast_in_dim.5), calls=%async_computation.3 | async-start | bytes 131072 | tf_op jit(solution)/shard_map/all_to_all | solution.py:28
  120.9 24.3 %all-to-all-start.5 = ((bf16[16,4,1792]{2,1,0:T(4,128)(2,1)}), bf16[16,4,1792]{2,1,0:T(4,128)(2,1)S(1)}, u32[]{:S(2)}, u32[]{:S(2)}) async-start(bf16[16,4,1792]{2,1,0:T(4,128)(2,1)} %reshape.54), calls=%async_computation.5 | async-start | bytes 458752 | tf_op jit(solution)/shard_map/all_to_all | solution.py:236
  131.0 3.3 %collective-permute-start.4 = (f32[]{:T(128)}, f32[]{:T(128)}, u32[]{:S(2)}, u32[]{:S(2)}) collective-permute-start(f32[]{:T(128)} %bitcast.9), channel_id=1, source_target_pairs={{0,64},{64,0},{1,65},{65,1},{2,66},{66,2},{3,67},{67,3},{4,68},{68... | collective-permute-start | bytes 20 | tf_op jit(solution)/shard_map/ppermute | solution.py:238

commit v3 on v2

v3 whole, which is shorter than its diff:
```python
import jax
import jax.numpy as jnp
from jax import lax
from jax.experimental import pallas as pl
from jax.experimental.pallas import tpu as pltpu
from jax.sharding import Mesh, PartitionSpec as P

GROUP_SIZE = 16
GROUPS = 2
ENTROPY_WEIGHT = 0.2
STEP = 256
Y, C, Z, X = 4, 2, 16, 4
VMEM = pl.BlockSpec(memory_space=pltpu.VMEM)
ANY = pl.BlockSpec(memory_space=pl.ANY)
PARAMS = pltpu.CompilerParams(vmem_limit_bytes=24 * 1024 * 1024)


def meta_kernel(offsets, lengths, groups, rewards, target_ref, out_ref):
    rollouts, rows = offsets.shape[0], out_ref.shape[1]
    per_tok = rows // Y
    place = lax.broadcasted_iota(jnp.int32, (1, rows), 1)
    row = (C * (place // per_tok) + lax.axis_index("c")) * per_tok + place % per_tok
    means = []
    for g in range(GROUPS):
        total = jnp.float32(0)
        for i in range(rollouts):
            total += jnp.where(groups[i] == g, rewards[i], jnp.float32(0))
        means.append(total / GROUP_SIZE)
    live = jnp.zeros((1, rows), jnp.float32)
    advantage = jnp.zeros((1, rows), jnp.float32)
    count = jnp.int32(0)
    for i in range(rollouts):
        first, length, mean = offsets[i], lengths[i], means[-1]
        for g in range(GROUPS - 1):
            mean = jnp.where(groups[i] == g, means[g], mean)
        member = jnp.where((row >= first) & (row < first + length), 1.0, 0.0)
        live += member
        advantage += member * (rewards[i] - mean)
        count += length
    weight = C * rows / jnp.full((1, rows), count, jnp.int32).astype(jnp.float32)
    out_ref[...] = jnp.concatenate(
        [live, advantage, weight, target_ref[...], jnp.zeros((4, rows), jnp.float32)], axis=0
    )


def row_meta(offsets, lengths, groups, rewards, target):
    smem = pl.BlockSpec(memory_space=pltpu.SMEM)
    return pl.pallas_call(
        meta_kernel,
        out_shape=jax.ShapeDtypeStruct((8, target.shape[1]), jnp.float32),
        in_specs=[smem] * 4 + [VMEM],
        out_specs=VMEM,
        compiler_params=PARAMS,
        name="row_meta",
    )(offsets, lengths, groups, rewards, target)


def merge(top, total, weighted, target):
    high = jnp.max(top, axis=0, keepdims=True)
    gap = top - high
    scale = jnp.exp(gap)
    return (
        high,
        jnp.sum(scale * total, axis=0, keepdims=True),
        jnp.sum(scale * (weighted + gap * total), axis=0, keepdims=True),
        jnp.sum(target, axis=0, keepdims=True),
    )


def merge_kernel(stats_ref, out_ref):
    parts = merge(*(stats_ref[:, i] for i in range(4)))
    block = jnp.concatenate([*parts, *parts], axis=0)
    for i in range(out_ref.shape[0]):
        out_ref[i] = block


def merged_stats(stats, copies):
    return pl.pallas_call(
        merge_kernel,
        out_shape=jax.ShapeDtypeStruct((copies, *stats.shape[1:]), jnp.float32),
        in_specs=[VMEM],
        out_specs=VMEM,
        compiler_params=PARAMS,
        name="merged_stats",
    )(stats)


def spread(block, axes, n):
    sent = jnp.broadcast_to(block[None], (n, *block.shape))
    return lax.all_to_all(sent, axes, 0, 0, tiled=True)


def x_neighbour(block, k):
    return lax.ppermute(block, "x", [((i + k) % X, i) for i in range(X)])


def first_column(chunk, vocab, width):
    y, c, z = (lax.axis_index(a) for a in ("y", "c", "z"))
    per_core = vocab // width
    other = chunk // per_core
    core = c + other * (1 - 2 * c)
    return ((2 * y + core) * Z + z) * vocab + (chunk % per_core) * width


def fetch_rows(parts, whole_ref, sem):
    size = parts[0].shape[0]
    copies = [
        pltpu.make_async_copy(part, whole_ref.at[i * size : (i + 1) * size], sem.at[i])
        for i, part in enumerate(parts)
    ]
    for copy in copies:
        copy.start()
    return copies


def logits_kernel(rows_ref, own_ref, *refs):
    *other_hbm, out_ref, other_ref, sem = refs
    fetch = fetch_rows(other_hbm, other_ref, sem)
    width = out_ref.shape[2]
    per_core = X // C
    for k in range(X):
        if k == per_core:
            for copy in fetch:
                copy.wait()
        w_ref = own_ref if k < per_core else other_ref
        at = k % per_core * width
        out_ref[k] = jnp.dot(
            rows_ref[...], w_ref[:, at : at + width], preferred_element_type=jnp.float32
        )


def partial_logits(rows, own, other):
    n, depth = rows.shape
    vocab = own.shape[1]
    width = C * vocab // X
    return pl.pallas_call(
        logits_kernel,
        out_shape=jax.ShapeDtypeStruct((X, n, width), jnp.float32),
        in_specs=[VMEM, VMEM] + [ANY] * len(other),
        out_specs=VMEM,
        scratch_shapes=[pltpu.VMEM(own.shape, own.dtype), pltpu.SemaphoreType.DMA((len(other),))],
        compiler_params=PARAMS,
        cost_estimate=pl.CostEstimate(
            flops=2 * n * depth * C * vocab, bytes_accessed=4 * X * n * width, transcendentals=0
        ),
        name="partial_logits",
    )(rows, own, *other)


def columns_of(values, n):
    row = lax.broadcasted_iota(jnp.int32, (128, n), 0)
    packed = jnp.zeros((128, n), jnp.float32)
    for i, value in enumerate(values):
        packed = jnp.where(row == i, value, packed)
    packed = packed.T
    return [packed[:, i : i + 1] for i in range(len(values))]


def stats_kernel(vocab, part_ref, meta_ref, logits_ref, stats_ref):
    logits = part_ref[0] + part_ref[1] + part_ref[2] + part_ref[3]
    logits_ref[...] = logits
    n, width = logits.shape
    top = jnp.max(logits, axis=1, keepdims=True)
    shifted = logits - top
    e = jnp.exp(shifted)
    column = lax.broadcasted_iota(jnp.int32, (n, width), 1) + first_column(lax.axis_index("x"), vocab, width)
    (target,) = columns_of([meta_ref[3:4, :n]], n)
    hit = column == target.astype(jnp.int32)
    values = (
        top,
        jnp.sum(e, axis=1, keepdims=True),
        jnp.sum(e * shifted, axis=1, keepdims=True),
        jnp.sum(jnp.where(hit, logits, 0.0), axis=1, keepdims=True),
    )
    lane = lax.broadcasted_iota(jnp.int32, (n, 128), 1)
    packed = jnp.zeros((n, 128), jnp.float32)
    for i, value in enumerate(values):
        packed = jnp.where(lane == i, value, packed)
    packed = packed.T[:8]
    for i in range(Z):
        stats_ref[i] = packed


def local_stats(part, meta, vocab):
    _, n, width = part.shape
    return pl.pallas_call(
        lambda *refs: stats_kernel(vocab, *refs),
        out_shape=(
            jax.ShapeDtypeStruct((n, width), jnp.float32),
            jax.ShapeDtypeStruct((Z, 8, n), jnp.float32),
        ),
        in_specs=[VMEM, VMEM],
        out_specs=(VMEM, VMEM),
        compiler_params=PARAMS,
        cost_estimate=pl.CostEstimate(
            flops=8 * n * width, bytes_accessed=4 * X * n * width, transcendentals=n * width
        ),
        name="local_stats",
    )(part, meta)


def grad_kernel(
    vocab, stats_ref, meta_ref, l0, l1, l2, l3, own_ref, *refs):
    *other_hbm, out_ref, loss_ref, g_ref, acc_ref, other_ref, sem = refs
    fetch = fetch_rows(other_hbm, other_ref, sem)
    n = l0.shape[0]
    top, total, weighted, target_value = merge(*(stats_ref[:, i] for i in range(4)))
    log_sum = jnp.log(total)
    log_total = top + log_sum
    entropy = log_sum - weighted / total
    live, advantage, weight, target = (meta_ref[i : i + 1] for i in range(4))
    row_loss = live * (-advantage * (target_value - log_total) - ENTROPY_WEIGHT * entropy)
    loss_ref[...] = weight[:, :1] * jnp.sum(row_loss, axis=1, keepdims=True)
    log_total, entropy, row_weight, advantage, target = columns_of(
        [log_total, entropy, weight * live, advantage, target], n
    )
    target = target.astype(jnp.int32)
    width = l0.shape[1]
    x = lax.axis_index("x")
    for k, l_ref in enumerate((l0, l1, l2, l3)):
        chunk = lax.rem(x + k, X)
        log_probability = l_ref[...] - log_total
        probability = jnp.exp(log_probability)
        column = lax.broadcasted_iota(jnp.int32, (n, width), 1) + first_column(chunk, vocab, width)
        hit = jnp.where(column == target, 1.0, 0.0)
        grad = row_weight * (
            advantage * (probability - hit)
            + ENTROPY_WEIGHT * probability * (log_probability + entropy)
        )
        g_ref[:, pl.ds(pl.multiple_of(chunk * width, width), width)] = grad.astype(jnp.bfloat16)
    contract = (((1,), (1,)), ((), ()))
    depth = own_ref.shape[0]
    for at in range(0, depth, STEP):
        acc_ref[:, at : at + STEP] = lax.dot_general(
            g_ref[:, :vocab], own_ref[at : at + STEP], contract, preferred_element_type=jnp.float32
        )
    for copy in fetch:
        copy.wait()
    for at in range(0, depth, STEP):
        part = acc_ref[:, at : at + STEP] + lax.dot_general(
            g_ref[:, vocab:], other_ref[at : at + STEP], contract, preferred_element_type=jnp.float32
        )
        out_ref[:, at : at + STEP] = part.astype(jnp.bfloat16)


def partial_grad(stats, meta, chunks, own, other):
    n, width = chunks[0].shape
    depth, vocab = own.shape
    return pl.pallas_call(
        lambda *refs: grad_kernel(vocab, *refs),
        out_shape=(
            jax.ShapeDtypeStruct((n, depth), jnp.bfloat16),
            jax.ShapeDtypeStruct((1, 1), jnp.float32),
        ),
        in_specs=[VMEM] * 7 + [ANY] * len(other),
        out_specs=(VMEM, VMEM),
        scratch_shapes=[
            pltpu.VMEM((n, C * vocab), jnp.bfloat16),
            pltpu.VMEM((n, depth), jnp.float32),
            pltpu.VMEM(own.shape, own.dtype),
            pltpu.SemaphoreType.DMA((len(other),)),
        ],
        compiler_params=PARAMS,
        cost_estimate=pl.CostEstimate(
            flops=2 * n * depth * C * vocab,
            bytes_accessed=4 * X * n * width,
            transcendentals=X * n * width,
        ),
        name="partial_grad",
    )(stats, meta, *chunks, own, *other)


def per_device(hidden, head_weight, targets, offsets, lengths, group_ids, rewards):
    c = lax.axis_index("c")
    depth, vocab = head_weight.shape
    total_rows = targets.shape[0]

    rows = total_rows // C
    per_tok = rows // Y
    own_targets = targets.astype(jnp.float32).reshape(Y, C, per_tok)[:, c].reshape(1, rows)
    meta = row_meta(offsets, lengths, group_ids, rewards, own_targets)

    swap = [(0, 1), (1, 0)]
    tok_rows = spread(hidden, "z", Z).reshape(per_tok, depth)
    other_weight = [lax.ppermute(w, "c", swap) for w in jnp.split(head_weight, 2)]
    tok_rows, meta = lax.optimization_barrier((tok_rows, meta))
    my_rows = lax.all_gather(tok_rows, "y", axis=0, tiled=True)

    part = partial_logits(my_rows, head_weight, other_weight)
    part = lax.all_to_all(part, "x", 0, 0, tiled=True)
    logits, stats = local_stats(part, meta, vocab)
    stats = lax.all_to_all(stats, "z", 0, 0, tiled=True)
    chunks = [logits, *(x_neighbour(logits, k) for k in range(1, X))]
    stats = lax.all_to_all(merged_stats(stats, Y * X), ("y", "x"), 0, 0, tiled=True)
    hidden_grad, loss = partial_grad(stats, meta, chunks, head_weight, other_weight)

    hidden_grad = lax.all_to_all(hidden_grad.reshape(Y, per_tok, depth), "y", 0, 0, tiled=True)
    hidden_grad = jnp.sum(hidden_grad.astype(jnp.float32), axis=0).astype(jnp.bfloat16)
    hidden_grad = lax.all_to_all(hidden_grad.reshape(Z, per_tok // Z, depth), "z", 0, 0, tiled=True)
    hidden_grad = jnp.sum(hidden_grad.astype(jnp.float32), axis=0)
    loss = loss[0, 0]
    return hidden_grad.astype(jnp.bfloat16), loss + lax.ppermute(loss, "c", swap)


def solution(mesh):
    split = Mesh(mesh.devices.reshape(Y, C, Z, X), ("y", "c", "z", "x"))
    voc = ("y", "c", "z")
    return jax.shard_map(
        per_device,
        mesh=split,
        in_specs=(P(voc, "x"), P("x", voc), P(), P(), P(), P(), P()),
        out_specs=(P(voc, "x"), P()),
        check_vma=False,
    )
```

time: 148 us -> 144 us (0.973)
  waiting for transfers between devices: 48.5 us -> 30.9 us
  blocking collectives: 26.9 us -> 44.4 us
  other arithmetic: 5.29 us -> 0.87 us
    all_to_all x0 -> x1, blocking collectives: none -> 17.3 us  [per_device(): part = lax.all_to_all(part, 'x', 0, 0, tiled=True)]
    all_to_all x2 -> x1, waiting for transfers between devices: 19.1 us -> 8.53 us  [spread(): return lax.all_to_all(sent, axes, 0, 0, tiled=True)]
    all_to_all x1, waiting for transfers between devices: 13.7 us -> 7.9 us  [per_device(): lax.all_to_all(merged_stats(stats, Y * X), ('y', 'x'), 0, 0, tiled=True)]
    all_to_all x2 -> x1, starting transfers between devices: 18.8 us -> 15.2 us  [spread(): return lax.all_to_all(sent, axes, 0, 0, tiled=True)]
    reduce_sum x5 -> x0, other arithmetic: 3.61 us -> none  [the longest x1 1.31 us: per_device(): weight_all = total_rows / jnp.sum(lengths).astype(jnp.float32)]
    ppermute x5 -> x6, starting transfers between devices: 12.3 us -> 15.4 us  [the longest x3 9.17 us: x_neighbour(): return lax.ppermute(block, 'x', [((i + k) % X, i) for i in range(X)])]
    split x0 -> x1, local copies, waits for them, and re-layouts: none -> 2.98 us  [per_device(): jnp.split(head_weight, 2)]
    pallas_call x0 -> x2, Pallas kernels: none -> 1.5 us  [the longest x1 0.78 us: row_meta(): pl.pallas_call(meta_kernel, out_shape=jax.ShapeDtypeStruct((8, target.sha...]
  transfers between devices with their start and end apart: 10 -> 10, of which waited for: 7 -> 6; matrix products, arithmetic and copies ran while one was open for 5% -> 2% of each run, Pallas kernels for 0% -> 1%
where the time goes in v3:
time: 144 us; the launch traced here: 143 us
  starting transfers between devices  50.5 us (35%)
  blocking collectives  44.4 us (31%)
  waiting for transfers between devices  30.9 us (21%)
  Pallas kernels  7.55 us (5%)
  local copies, waits for them, and re-layouts  5.49 us (4%)
  between operations  3.28 us (2%)
    all_to_all x1, blocking collectives, per_device(): part = lax.all_to_all(part, 'x', 0, 0, tiled=True)  17.3 us
    all_to_all x1, starting transfers between devices, spread(): return lax.all_to_all(sent, axes, 0, 0, tiled=True)  15.2 us
    all_gather x1, blocking collectives, per_device(): my_rows = lax.all_gather(tok_rows, 'y', axis=0, tiled=True)  14.5 us
    all_to_all x1, blocking collectives, per_device(): lax.all_to_all(hidden_grad.reshape(Y, per_tok, depth), 'y', 0, 0, tiled=T...  12.6 us
    all_to_all x1, starting transfers between devices, per_device(): lax.all_to_all(hidden_grad.reshape(Z, per_tok // Z, depth), 'z', 0, 0, ti...  10.2 us
    all_to_all x1, waiting for transfers between devices, per_device(): lax.all_to_all(hidden_grad.reshape(Z, per_tok // Z, depth), 'z', 0, 0, ti...  9.77 us
    ppermute x3, starting transfers between devices, x_neighbour(): return lax.ppermute(block, 'x', [((i + k) % X, i) for i in range(X)])  9.17 us
    all_to_all x1, waiting for transfers between devices, spread(): return lax.all_to_all(sent, axes, 0, 0, tiled=True)  8.53 us
  transfers between devices with their start and end apart: 10, of which 6 were waited for; matrix products, arithmetic and copies ran while one was open for 2% of the time, Pallas kernels for 1%

profile of v3, /device:TPU:32, one launch (start us, length us, event | category | flops | bytes accessed | tf_op | source)
XLA Modules:
  0.0 143.0 jit_solution(2487232212967172989)
XLA Ops:
  0.6 1.5 %broadcast_in_dim.2 = bf16[16,4,1792]{2,1,0:T(4,128)(2,1)} broadcast(bf16[4,1792]{1,0:T(4,128)(2,1)} %param.7), dimensions={1,2} | broadcast | bytes 243712 | tf_op jit(solution)/shard_map/broadcast_in_dim | solution.py:89
  2.1 15.2 %all-to-all-start = ((bf16[16,4,1792]{2,1,0:T(4,128)(2,1)}), bf16[16,4,1792]{2,1,0:T(4,128)(2,1)S(1)}, u32[]{:S(2)}, u32[]{:S(2)}) async-start(bf16[16,4,1792]{2,1,0:T(4,128)(2,1)} %broadcast_in_dim.2), calls=%async_computation | async-start | bytes 458752 | tf_op jit(solution)/shard_map/all_to_all | solution.py:90
  17.4 3.0 %fusion = (bf16[896,512]{1,0:T(8,128)(2,1)}, bf16[896,512]{1,0:T(8,128)(2,1)}) fusion(bf16[1792,512]{1,0:T(8,128)(2,1)} %refs_6_.1), kind=kLoop, calls=%fused_computation.1 | loop fusion | bytes 3670016 | tf_op jit(solution)/shard_map/split | solution.py:285
  20.4 1.9 %collective-permute-start.1 = (bf16[896,512]{1,0:T(8,128)(2,1)}, bf16[896,512]{1,0:T(8,128)(2,1)S(1)}, u32[]{:S(2)}, u32[]{:S(2)}) collective-permute-start(bf16[896,512]{1,0:T(8,128)(2,1)} %get-tuple-element.14), channel_id=1, source_target_pairs={{0,64},{64,0},{1,65},{65,1},{2,66},{66,2},{3,67},{67,3},{4,68},{68... | collective-permute-start | bytes 2752520 | tf_op jit(solution)/shard_map/ppermute | solution.py:285
  22.3 2.4 %collective-permute-start = (bf16[896,512]{1,0:T(8,128)(2,1)}, bf16[896,512]{1,0:T(8,128)(2,1)}, u32[]{:S(2)}, u32[]{:S(2)}) collective-permute-start(bf16[896,512]{1,0:T(8,128)(2,1)} %get-tuple-element.15), channel_id=1, source_target_pairs={{0,64},{64,0},{1,65},{65,1},{2,66},{66,2},{3,67},{67,3},{4,68},{68... | collective-permute-start | bytes 2752520 | tf_op jit(solution)/shard_map/ppermute | solution.py:285
  24.7 0.1 reshape.18
  24.8 0.1 reshape_squeeze.3.target_ref
  24.9 0.8 row_meta.1.refs_1_
  25.7 8.5 %all-to-all-done = bf16[16,4,1792]{2,1,0:T(4,128)(2,1)S(1)} async-done(((bf16[16,4,1792]{2,1,0:T(4,128)(2,1)}), bf16[16,4,1792]{2,1,0:T(4,128)(2,1)S(1)}, u32[]{:S(2)}, u32[]{:S(2)}) %all-to-all-start) | async-done | bytes 229408 | tf_op jit(solution)/shard_map/all_to_all | solution.py:90
  34.2 0.1 reshape.17
  34.3 14.5 %all_gather.3.rows_ref = bf16[256,1792]{1,0:T(8,128)(2,1)S(1)} all-gather(bf16[64,1792]{1,0:T(8,128)(2,1)S(1)} %reshape.17), channel_id=1, replica_groups=mesh['y'=4,'c'=2,'z'=16,'x'=4] {'y'}, dimensions={0}, use_global_device_ids=true | all-gather | bytes 1146880 | tf_op jit(solution)/shard_map/all_gather | solution.py:287
  48.8 1.8 %partial_logits.1 = f32[4,256,256]{2,1,0:T(8,128)S(1)} custom-call(bf16[256,1792]{1,0:T(8,128)(2,1)S(1)} %all_gather.3.rows_ref, bf16[1792,512]{1,0:T(8,128)(2,1)S(1)} %copy-done, bf16[896,512]{1,0:T(8,128)(2,1)} %collective-permute-done.refs_0_.refs_7_, bf16[896,512]{1,0:T(8,128)(2,1)S(1)} %collective-permute-done.1.refs_1_.refs_8_), custom_call_target="tpu_custom_call" | custom-call | flops 939524096 | bytes 1048576 | tf_op jit(solution)/shard_map/partial_logits/pallas_call | solution.py:136
  50.6 17.3 %all_to_all.30.refs_0_ = f32[4,256,256]{2,1,0:T(8,128)S(1)} all-to-all(f32[4,256,256]{2,1,0:T(8,128)S(1)} %partial_logits.1), channel_id=1, replica_groups=mesh['y'=4,'c'=2,'z'=16,'x'=4] {'x'}, dimensions={0} | all-to-all | bytes 2097152 | tf_op jit(solution)/shard_map/all_to_all | solution.py:290
  67.9 1.1 local_stats.1
  69.0 6.2 %all-to-all-start.2 = ((f32[16,8,256]{2,1,0:T(8,128)}), f32[16,8,256]{2,1,0:T(8,128)S(1)}, u32[]{:S(2)}, u32[]{:S(2)}) async-start(f32[16,8,256]{2,1,0:T(8,128)} %get-tuple-element.10), calls=%async_computation.2 | async-start | bytes 262144 | tf_op jit(solution)/shard_map/all_to_all | solution.py:292
  75.2 2.5 %collective-permute-start.4 = (f32[256,256]{1,0:T(8,128)S(1)}, f32[256,256]{1,0:T(8,128)S(1)}, u32[]{:S(2)}, u32[]{:S(2)}) collective-permute-start(f32[256,256]{1,0:T(8,128)S(1)} %get-tuple-element.11.refs_2_), channel_id=1, source_target_pairs={{3,0},{0,1},{1,2},{2,3},{7,4},{4,5},{5,6},{6,7},{11,8},{8,9},{9,10... | collective-permute-start | bytes 786440 | tf_op jit(solution)/shard_map/ppermute | solution.py:94
  77.7 4.0 %collective-permute-start.3 = (f32[256,256]{1,0:T(8,128)S(1)}, f32[256,256]{1,0:T(8,128)}, u32[]{:S(2)}, u32[]{:S(2)}) collective-permute-start(f32[256,256]{1,0:T(8,128)S(1)} %get-tuple-element.11.refs_2_), channel_id=1, source_target_pairs={{2,0},{3,1},{0,2},{1,3},{6,4},{7,5},{4,6},{5,7},{10,8},{11,9},{8,1... | collective-permute-start | bytes 786440 | tf_op jit(solution)/shard_map/ppermute | solution.py:94
  81.7 2.7 %collective-permute-start.2 = (f32[256,256]{1,0:T(8,128)S(1)}, f32[256,256]{1,0:T(8,128)}, u32[]{:S(2)}, u32[]{:S(2)}) collective-permute-start(f32[256,256]{1,0:T(8,128)S(1)} %get-tuple-element.11.refs_2_), channel_id=1, source_target_pairs={{1,0},{2,1},{3,2},{0,3},{5,4},{6,5},{7,6},{4,7},{9,8},{10,9},{11,1... | collective-permute-start | bytes 786440 | tf_op jit(solution)/shard_map/ppermute | solution.py:94
  84.4 3.5 %all-to-all-done.2.stats_ref = f32[16,8,256]{2,1,0:T(8,128)S(1)} async-done(((f32[16,8,256]{2,1,0:T(8,128)}), f32[16,8,256]{2,1,0:T(8,128)S(1)}, u32[]{:S(2)}, u32[]{:S(2)}) %all-to-all-start.2) | async-done | bytes 131104 | tf_op jit(solution)/shard_map/all_to_all | solution.py:292
  87.8 0.7 merged_stats.1
  88.6 3.5 %all-to-all-start.3 = ((f32[16,8,256]{2,1,0:T(8,128)}), f32[16,8,256]{2,1,0:T(8,128)S(1)}, u32[]{:S(2)}, u32[]{:S(2)}) async-start(f32[16,8,256]{2,1,0:T(8,128)} %merged_stats.1), calls=%async_computation.3 | async-start | bytes 262144 | tf_op jit(solution)/shard_map/all_to_all | solution.py:294
  92.1 0.1 collective-permute-done.2.refs_3_
  92.2 7.9 %all-to-all-done.3.refs_0_ = f32[16,8,256]{2,1,0:T(8,128)S(1)} async-done(((f32[16,8,256]{2,1,0:T(8,128)}), f32[16,8,256]{2,1,0:T(8,128)S(1)}, u32[]{:S(2)}, u32[]{:S(2)}) %all-to-all-start.3) | async-done | bytes 131104 | tf_op jit(solution)/shard_map/all_to_all | solution.py:294
  100.1 3.2 %partial_grad.1 = (bf16[256,1792]{1,0:T(8,128)(2,1)S(1)}, f32[1,1]{1,0:T(1,128)}) custom-call(f32[16,8,256]{2,1,0:T(8,128)S(1)} %all-to-all-done.3.refs_0_, f32[8,256]{1,0:T(8,128)S(1)} %row_meta.1.refs_1_, f32[256,256]{1,0:T(8,128)S(1)} %get-tuple-element.11.refs_2_, f32[256,256]{1,0:T(8,128)} %collective-permute-done.2.refs_3_, ...), custom_call_target="tpu_custom_call" | custom-call | flops 939524096 | bytes 1048576 | tf_op jit(solution)/shard_map/partial_grad/pallas_call | solution.py:249
  103.2 12.6 %all_to_all.31 = bf16[4,64,1792]{2,1,0:T(8,128)(2,1)S(1)} all-to-all(bf16[4,64,1792]{2,1,0:T(8,128)(2,1)S(1)} %bitcast.2), channel_id=1, replica_groups=mesh['y'=4,'c'=2,'z'=16,'x'=4] {'y'}, dimensions={0} | all-to-all | bytes 1835008 | tf_op jit(solution)/shard_map/all_to_all | solution.py:297
  115.8 0.2 reduce_sum.24
  116.0 0.7 reshape.20
  116.7 10.2 %all-to-all-start.5 = ((bf16[16,4,1792]{2,1,0:T(4,128)(2,1)}), bf16[16,4,1792]{2,1,0:T(4,128)(2,1)S(1)}, u32[]{:S(2)}, u32[]{:S(2)}) async-start(bf16[16,4,1792]{2,1,0:T(4,128)(2,1)} %reshape.20), calls=%async_computation.5 | async-start | bytes 458752 | tf_op jit(solution)/shard_map/all_to_all | solution.py:299
  126.9 1.9 %collective-permute-start.5 = (f32[]{:T(128)}, f32[]{:T(128)}, u32[]{:S(2)}, u32[]{:S(2)}) collective-permute-start(f32[]{:T(128)} %bitcast.1), channel_id=1, source_target_pairs={{0,64},{64,0},{1,65},{65,1},{2,66},{66,2},{3,67},{67,3},{4,68},{68... | collective-permute-start | bytes 20 | tf_op jit(solution)/shard_map/ppermute | solution.py:302
  128.9 1.2 collective-permute-done.5
  131.4 9.8 %all-to-all-done.5 = bf16[16,4,1792]{2,1,0:T(4,128)(2,1)S(1)} async-done(((bf16[16,4,1792]{2,1,0:T(4,128)(2,1)}), bf16[16,4,1792]{2,1,0:T(4,128)(2,1)S(1)}, u32[]{:S(2)}, u32[]{:S(2)}) %all-to-all-start.5) | async-done | bytes 229408 | tf_op jit(solution)/shard_map/all_to_all | solution.py:299
  141.2 0.7 reduce_sum.25
  (18 shorter events, 0.1 us)
Async XLA Ops:
  2.1 32.1 %all-to-all-start = ((bf16[16,4,1792]{2,1,0:T(4,128)(2,1)}), bf16[16,4,1792]{2,1,0:T(4,128)(2,1)S(1)}, u32[]{:S(2)}, u32[]{:S(2)}) async-start(bf16[16,4,1792]{2,1,0:T(4,128)(2,1)} %broadcast_in_dim.2), calls=%async_computation | async-start | bytes 458752 | tf_op jit(solution)/shard_map/all_to_all | solution.py:90
  17.3 7.4 %copy-start.5 = (s32[512]{0:T(512)S(1)}, s32[512]{0:T(512)}, u32[]{:S(2)}) copy-start(s32[512]{0:T(512)} %param.9) | copy-start | bytes 6148
  17.3 7.6 %copy-start.1 = (s32[32]{0:T(128)S(1)}, s32[32]{0:T(128)}, u32[]{:S(2)}) copy-start(s32[32]{0:T(128)} %offsets.1) | copy-start | bytes 388
  17.3 7.6 %copy-start.2 = (s32[32]{0:T(128)S(1)}, s32[32]{0:T(128)}, u32[]{:S(2)}) copy-start(s32[32]{0:T(128)} %lengths.1) | copy-start | bytes 388
  17.4 7.6 %copy-start.3 = (s32[32]{0:T(128)S(1)}, s32[32]{0:T(128)}, u32[]{:S(2)}) copy-start(s32[32]{0:T(128)} %groups.1) | copy-start | bytes 388
  17.4 7.6 %copy-start.4 = (f32[32]{0:T(128)S(1)}, f32[32]{0:T(128)}, u32[]{:S(2)}) copy-start(f32[32]{0:T(128)} %rewards.1) | copy-start | bytes 388
  17.4 31.4 %copy-start = (bf16[1792,512]{1,0:T(8,128)(2,1)S(1)}, bf16[1792,512]{1,0:T(8,128)(2,1)}, u32[]{:S(2)}) copy-start(bf16[1792,512]{1,0:T(8,128)(2,1)} %refs_6_.1) | copy-start | bytes 5505028
  20.4 28.4 %collective-permute-start.1 = (bf16[896,512]{1,0:T(8,128)(2,1)}, bf16[896,512]{1,0:T(8,128)(2,1)S(1)}, u32[]{:S(2)}, u32[]{:S(2)}) collective-permute-start(bf16[896,512]{1,0:T(8,128)(2,1)} %get-tuple-element.14), channel_id=1, source_target_pairs={{0,64},{64,0},{1,65},{65,1},{2,66},{66,2},{3,67},{67,3},{4,68},{68... | collective-permute-start | bytes 2752520 | tf_op jit(solution)/shard_map/ppermute | solution.py:285
  22.3 26.5 %collective-permute-start = (bf16[896,512]{1,0:T(8,128)(2,1)}, bf16[896,512]{1,0:T(8,128)(2,1)}, u32[]{:S(2)}, u32[]{:S(2)}) collective-permute-start(bf16[896,512]{1,0:T(8,128)(2,1)} %get-tuple-element.15), channel_id=1, source_target_pairs={{0,64},{64,0},{1,65},{65,1},{2,66},{66,2},{3,67},{67,3},{4,68},{68... | collective-permute-start | bytes 2752520 | tf_op jit(solution)/shard_map/ppermute | solution.py:285
  69.0 18.8 %all-to-all-start.2 = ((f32[16,8,256]{2,1,0:T(8,128)}), f32[16,8,256]{2,1,0:T(8,128)S(1)}, u32[]{:S(2)}, u32[]{:S(2)}) async-start(f32[16,8,256]{2,1,0:T(8,128)} %get-tuple-element.10), calls=%async_computation.2 | async-start | bytes 262144 | tf_op jit(solution)/shard_map/all_to_all | solution.py:292
  75.2 16.9 %collective-permute-start.4 = (f32[256,256]{1,0:T(8,128)S(1)}, f32[256,256]{1,0:T(8,128)S(1)}, u32[]{:S(2)}, u32[]{:S(2)}) collective-permute-start(f32[256,256]{1,0:T(8,128)S(1)} %get-tuple-element.11.refs_2_), channel_id=1, source_target_pairs={{3,0},{0,1},{1,2},{2,3},{7,4},{4,5},{5,6},{6,7},{11,8},{8,9},{9,10... | collective-permute-start | bytes 786440 | tf_op jit(solution)/shard_map/ppermute | solution.py:94
  77.7 14.4 %collective-permute-start.3 = (f32[256,256]{1,0:T(8,128)S(1)}, f32[256,256]{1,0:T(8,128)}, u32[]{:S(2)}, u32[]{:S(2)}) collective-permute-start(f32[256,256]{1,0:T(8,128)S(1)} %get-tuple-element.11.refs_2_), channel_id=1, source_target_pairs={{2,0},{3,1},{0,2},{1,3},{6,4},{7,5},{4,6},{5,7},{10,8},{11,9},{8,1... | collective-permute-start | bytes 786440 | tf_op jit(solution)/shard_map/ppermute | solution.py:94
  81.7 10.5 %collective-permute-start.2 = (f32[256,256]{1,0:T(8,128)S(1)}, f32[256,256]{1,0:T(8,128)}, u32[]{:S(2)}, u32[]{:S(2)}) collective-permute-start(f32[256,256]{1,0:T(8,128)S(1)} %get-tuple-element.11.refs_2_), channel_id=1, source_target_pairs={{1,0},{2,1},{3,2},{0,3},{5,4},{6,5},{7,6},{4,7},{9,8},{10,9},{11,1... | collective-permute-start | bytes 786440 | tf_op jit(solution)/shard_map/ppermute | solution.py:94
  88.6 11.5 %all-to-all-start.3 = ((f32[16,8,256]{2,1,0:T(8,128)}), f32[16,8,256]{2,1,0:T(8,128)S(1)}, u32[]{:S(2)}, u32[]{:S(2)}) async-start(f32[16,8,256]{2,1,0:T(8,128)} %merged_stats.1), calls=%async_computation.3 | async-start | bytes 262144 | tf_op jit(solution)/shard_map/all_to_all | solution.py:294
  116.7 24.4 %all-to-all-start.5 = ((bf16[16,4,1792]{2,1,0:T(4,128)(2,1)}), bf16[16,4,1792]{2,1,0:T(4,128)(2,1)S(1)}, u32[]{:S(2)}, u32[]{:S(2)}) async-start(bf16[16,4,1792]{2,1,0:T(4,128)(2,1)} %reshape.20), calls=%async_computation.5 | async-start | bytes 458752 | tf_op jit(solution)/shard_map/all_to_all | solution.py:299
  126.9 3.1 %collective-permute-start.5 = (f32[]{:T(128)}, f32[]{:T(128)}, u32[]{:S(2)}, u32[]{:S(2)}) collective-permute-start(f32[]{:T(128)} %bitcast.1), channel_id=1, source_target_pairs={{0,64},{64,0},{1,65},{65,1},{2,66},{66,2},{3,67},{67,3},{4,68},{68... | collective-permute-start | bytes 20 | tf_op jit(solution)/shard_map/ppermute | solution.py:302

commit v4 on v3

--- a/solution.py
+++ b/solution.py
@@ -199,27 +199,52 @@
     )(part, meta)
 
 
-def grad_kernel(
-    vocab, stats_ref, meta_ref, l0, l1, l2, l3, own_ref, *refs):
-    *other_hbm, out_ref, loss_ref, g_ref, acc_ref, other_ref, sem = refs
+def row_terms(stats_ref):
+    top, total, weighted, target = merge(*(stats_ref[:, i] for i in range(4)))
+    log_sum = jnp.log(total)
+    return top + log_sum, log_sum - weighted / total, target
+
+
+def loss_kernel(stats_ref, meta_ref, out_ref):
+    log_total, entropy, target = row_terms(stats_ref)
+    live, advantage, weight = (meta_ref[i : i + 1] for i in range(3))
+    row_loss = live * (-advantage * (target - log_total) - ENTROPY_WEIGHT * entropy)
+    out_ref[...] = weight[:, :1] * jnp.sum(row_loss, axis=1, keepdims=True)
+
+
+def rows_loss(stats, meta):
+    return pl.pallas_call(
+        loss_kernel,
+        out_shape=jax.ShapeDtypeStruct((1, 1), jnp.float32),
+        in_specs=[VMEM, VMEM],
+        out_specs=VMEM,
+        compiler_params=PARAMS,
+        name="rows_loss",
+    )(stats, meta)
+
+
+def grad_kernel(vocab, stats_ref, meta_ref, l0, l1, l2, l3, own_ref, *refs):
+    *other_hbm, out_ref, g_ref, acc_ref, other_ref, l_ref, sem, move_sem = refs
+    x = lax.axis_index("x")
+    moves = [
+        pltpu.make_async_copy(ref, l_ref.at[lax.rem(x + k, X)], move_sem.at[k])
+        for k, ref in enumerate((l0, l1, l2, l3))
+    ]
+    for copy in moves:
+        copy.start()
     fetch = fetch_rows(other_hbm, other_ref, sem)
     n = l0.shape[0]
-    top, total, weighted, target_value = merge(*(stats_ref[:, i] for i in range(4)))
-    log_sum = jnp.log(total)
-    log_total = top + log_sum
-    entropy = log_sum - weighted / total
+    log_total, entropy, _ = row_terms(stats_ref)
     live, advantage, weight, target = (meta_ref[i : i + 1] for i in range(4))
-    row_loss = live * (-advantage * (target_value - log_total) - ENTROPY_WEIGHT * entropy)
-    loss_ref[...] = weight[:, :1] * jnp.sum(row_loss, axis=1, keepdims=True)
     log_total, entropy, row_weight, advantage, target = columns_of(
         [log_total, entropy, weight * live, advantage, target], n
     )
     target = target.astype(jnp.int32)
     width = l0.shape[1]
-    x = lax.axis_index("x")
-    for k, l_ref in enumerate((l0, l1, l2, l3)):
-        chunk = lax.rem(x + k, X)
-        log_probability = l_ref[...] - log_total
+    for copy in moves:
+        copy.wait()
+    for chunk in range(X):
+        log_probability = l_ref[chunk] - log_total
         probability = jnp.exp(log_probability)
         column = lax.broadcasted_iota(jnp.int32, (n, width), 1) + first_column(chunk, vocab, width)
         hit = jnp.where(column == target, 1.0, 0.0)
@@ -227,7 +252,7 @@
             advantage * (probability - hit)
             + ENTROPY_WEIGHT * probability * (log_probability + entropy)
         )
-        g_ref[:, pl.ds(pl.multiple_of(chunk * width, width), width)] = grad.astype(jnp.bfloat16)
+        g_ref[:, chunk * width : (chunk + 1) * width] = grad.astype(jnp.bfloat16)
     contract = (((1,), (1,)), ((), ()))
     depth = own_ref.shape[0]
     for at in range(0, depth, STEP):
@@ -248,17 +273,16 @@
     depth, vocab = own.shape
     return pl.pallas_call(
         lambda *refs: grad_kernel(vocab, *refs),
-        out_shape=(
-            jax.ShapeDtypeStruct((n, depth), jnp.bfloat16),
-            jax.ShapeDtypeStruct((1, 1), jnp.float32),
-        ),
-        in_specs=[VMEM] * 7 + [ANY] * len(other),
-        out_specs=(VMEM, VMEM),
+        out_shape=jax.ShapeDtypeStruct((n, depth), jnp.bfloat16),
+        in_specs=[VMEM] * 2 + [ANY] * X + [VMEM] + [ANY] * len(other),
+        out_specs=VMEM,
         scratch_shapes=[
             pltpu.VMEM((n, C * vocab), jnp.bfloat16),
             pltpu.VMEM((n, depth), jnp.float32),
             pltpu.VMEM(own.shape, own.dtype),
+            pltpu.VMEM((X, n, width), jnp.float32),
             pltpu.SemaphoreType.DMA((len(other),)),
+            pltpu.SemaphoreType.DMA((X,)),
         ],
         compiler_params=PARAMS,
         cost_estimate=pl.CostEstimate(
@@ -292,13 +316,13 @@
     stats = lax.all_to_all(stats, "z", 0, 0, tiled=True)
     chunks = [logits, *(x_neighbour(logits, k) for k in range(1, X))]
     stats = lax.all_to_all(merged_stats(stats, Y * X), ("y", "x"), 0, 0, tiled=True)
-    hidden_grad, loss = partial_grad(stats, meta, chunks, head_weight, other_weight)
+    hidden_grad = partial_grad(stats, meta, chunks, head_weight, other_weight)
 
     hidden_grad = lax.all_to_all(hidden_grad.reshape(Y, per_tok, depth), "y", 0, 0, tiled=True)
     hidden_grad = jnp.sum(hidden_grad.astype(jnp.float32), axis=0).astype(jnp.bfloat16)
     hidden_grad = lax.all_to_all(hidden_grad.reshape(Z, per_tok // Z, depth), "z", 0, 0, tiled=True)
     hidden_grad = jnp.sum(hidden_grad.astype(jnp.float32), axis=0)
-    loss = loss[0, 0]
+    loss = rows_loss(stats, meta)[0, 0]
     return hidden_grad.astype(jnp.bfloat16), loss + lax.ppermute(loss, "c", swap)
 
 

time: 144 us -> 144 us (level)
    pallas_call x1 -> x2, Pallas kernels: 3.16 us -> 3.48 us  [the longest x1 2.83 us: partial_grad(): pl.pallas_call(lambda *refs: grad_kernel(vocab, *refs), out_shape=jax.Sha...]
  transfers between devices with their start and end apart: 10 -> 10, of which waited for: 6 -> 6; matrix products, arithmetic and copies ran while one was open for 2% -> 2% of each run, Pallas kernels for 1% -> 2%
where the time goes in v4:
time: 144 us; the launch traced here: 143 us
  starting transfers between devices  50.5 us (35%)
  blocking collectives  44.4 us (31%)
  waiting for transfers between devices  30.3 us (21%)
  Pallas kernels  7.87 us (5%)
  local copies, waits for them, and re-layouts  5.49 us (4%)
  between operations  3.27 us (2%)
    all_to_all x1, blocking collectives, per_device(): part = lax.all_to_all(part, 'x', 0, 0, tiled=True)  17.3 us
    all_to_all x1, starting transfers between devices, spread(): return lax.all_to_all(sent, axes, 0, 0, tiled=True)  15.2 us
    all_gather x1, blocking collectives, per_device(): my_rows = lax.all_gather(tok_rows, 'y', axis=0, tiled=True)  14.5 us
    all_to_all x1, blocking collectives, per_device(): lax.all_to_all(hidden_grad.reshape(Y, per_tok, depth), 'y', 0, 0, tiled=T...  12.6 us
    all_to_all x1, starting transfers between devices, per_device(): lax.all_to_all(hidden_grad.reshape(Z, per_tok // Z, depth), 'z', 0, 0, ti...  10.2 us
    ppermute x3, starting transfers between devices, x_neighbour(): return lax.ppermute(block, 'x', [((i + k) % X, i) for i in range(X)])  9.17 us
    all_to_all x1, waiting for transfers between devices, per_device(): lax.all_to_all(hidden_grad.reshape(Z, per_tok // Z, depth), 'z', 0, 0, ti...  9.13 us
    all_to_all x1, waiting for transfers between devices, spread(): return lax.all_to_all(sent, axes, 0, 0, tiled=True)  8.54 us
  transfers between devices with their start and end apart: 10, of which 6 were waited for; matrix products, arithmetic and copies ran while one was open for 2% of the time, Pallas kernels for 2%

profile of v4, /device:TPU:32, one launch (start us, length us, event | category | flops | bytes accessed | tf_op | source)
XLA Modules:
  0.0 142.7 jit_solution(1003762575702611268)
XLA Ops:
  0.6 1.5 %broadcast_in_dim.2 = bf16[16,4,1792]{2,1,0:T(4,128)(2,1)} broadcast(bf16[4,1792]{1,0:T(4,128)(2,1)} %param.7), dimensions={1,2} | broadcast | bytes 243712 | tf_op jit(solution)/shard_map/broadcast_in_dim | solution.py:89
  2.1 15.2 %all-to-all-start = ((bf16[16,4,1792]{2,1,0:T(4,128)(2,1)}), bf16[16,4,1792]{2,1,0:T(4,128)(2,1)S(1)}, u32[]{:S(2)}, u32[]{:S(2)}) async-start(bf16[16,4,1792]{2,1,0:T(4,128)(2,1)} %broadcast_in_dim.2), calls=%async_computation | async-start | bytes 458752 | tf_op jit(solution)/shard_map/all_to_all | solution.py:90
  17.4 3.0 %fusion = (bf16[896,512]{1,0:T(8,128)(2,1)}, bf16[896,512]{1,0:T(8,128)(2,1)}) fusion(bf16[1792,512]{1,0:T(8,128)(2,1)} %refs_6_.1), kind=kLoop, calls=%fused_computation.1 | loop fusion | bytes 3670016 | tf_op jit(solution)/shard_map/split | solution.py:309
  20.4 1.9 %collective-permute-start.1 = (bf16[896,512]{1,0:T(8,128)(2,1)}, bf16[896,512]{1,0:T(8,128)(2,1)S(1)}, u32[]{:S(2)}, u32[]{:S(2)}) collective-permute-start(bf16[896,512]{1,0:T(8,128)(2,1)} %get-tuple-element.10), channel_id=1, source_target_pairs={{0,64},{64,0},{1,65},{65,1},{2,66},{66,2},{3,67},{67,3},{4,68},{68... | collective-permute-start | bytes 2752520 | tf_op jit(solution)/shard_map/ppermute | solution.py:309
  22.3 2.4 %collective-permute-start = (bf16[896,512]{1,0:T(8,128)(2,1)}, bf16[896,512]{1,0:T(8,128)(2,1)}, u32[]{:S(2)}, u32[]{:S(2)}) collective-permute-start(bf16[896,512]{1,0:T(8,128)(2,1)} %get-tuple-element.11), channel_id=1, source_target_pairs={{0,64},{64,0},{1,65},{65,1},{2,66},{66,2},{3,67},{67,3},{4,68},{68... | collective-permute-start | bytes 2752520 | tf_op jit(solution)/shard_map/ppermute | solution.py:309
  24.7 0.1 reshape.18
  24.8 0.1 reshape_squeeze.3.target_ref
  24.9 0.8 row_meta.1.refs_1_.meta_ref
  25.7 8.5 %all-to-all-done = bf16[16,4,1792]{2,1,0:T(4,128)(2,1)S(1)} async-done(((bf16[16,4,1792]{2,1,0:T(4,128)(2,1)}), bf16[16,4,1792]{2,1,0:T(4,128)(2,1)S(1)}, u32[]{:S(2)}, u32[]{:S(2)}) %all-to-all-start) | async-done | bytes 229408 | tf_op jit(solution)/shard_map/all_to_all | solution.py:90
  34.2 0.1 reshape.17
  34.3 14.5 %all_gather.3.rows_ref = bf16[256,1792]{1,0:T(8,128)(2,1)S(1)} all-gather(bf16[64,1792]{1,0:T(8,128)(2,1)S(1)} %reshape.17), channel_id=1, replica_groups=mesh['y'=4,'c'=2,'z'=16,'x'=4] {'y'}, dimensions={0}, use_global_device_ids=true | all-gather | bytes 1146880 | tf_op jit(solution)/shard_map/all_gather | solution.py:311
  48.8 1.8 %partial_logits.1 = f32[4,256,256]{2,1,0:T(8,128)S(1)} custom-call(bf16[256,1792]{1,0:T(8,128)(2,1)S(1)} %all_gather.3.rows_ref, bf16[1792,512]{1,0:T(8,128)(2,1)S(1)} %copy-done, bf16[896,512]{1,0:T(8,128)(2,1)} %collective-permute-done.refs_0_.refs_7_, bf16[896,512]{1,0:T(8,128)(2,1)S(1)} %collective-permute-done.1.refs_1_.refs_8_), custom_call_target="tpu_custom_call" | custom-call | flops 939524096 | bytes 1048576 | tf_op jit(solution)/shard_map/partial_logits/pallas_call | solution.py:136
  50.6 17.3 %all_to_all.30.refs_0_ = f32[4,256,256]{2,1,0:T(8,128)S(1)} all-to-all(f32[4,256,256]{2,1,0:T(8,128)S(1)} %partial_logits.1), channel_id=1, replica_groups=mesh['y'=4,'c'=2,'z'=16,'x'=4] {'x'}, dimensions={0} | all-to-all | bytes 2097152 | tf_op jit(solution)/shard_map/all_to_all | solution.py:314
  67.9 1.0 local_stats.1
  69.0 6.2 %all-to-all-start.2 = ((f32[16,8,256]{2,1,0:T(8,128)}), f32[16,8,256]{2,1,0:T(8,128)S(1)}, u32[]{:S(2)}, u32[]{:S(2)}) async-start(f32[16,8,256]{2,1,0:T(8,128)} %get-tuple-element.8), calls=%async_computation.2 | async-start | bytes 262144 | tf_op jit(solution)/shard_map/all_to_all | solution.py:316
  75.2 2.5 %collective-permute-start.4 = (f32[256,256]{1,0:T(8,128)S(1)}, f32[256,256]{1,0:T(8,128)S(1)}, u32[]{:S(2)}, u32[]{:S(2)}) collective-permute-start(f32[256,256]{1,0:T(8,128)S(1)} %get-tuple-element.9.refs_2_), channel_id=1, source_target_pairs={{3,0},{0,1},{1,2},{2,3},{7,4},{4,5},{5,6},{6,7},{11,8},{8,9},{9,10... | collective-permute-start | bytes 786440 | tf_op jit(solution)/shard_map/ppermute | solution.py:94
  77.7 4.0 %collective-permute-start.3 = (f32[256,256]{1,0:T(8,128)S(1)}, f32[256,256]{1,0:T(8,128)}, u32[]{:S(2)}, u32[]{:S(2)}) collective-permute-start(f32[256,256]{1,0:T(8,128)S(1)} %get-tuple-element.9.refs_2_), channel_id=1, source_target_pairs={{2,0},{3,1},{0,2},{1,3},{6,4},{7,5},{4,6},{5,7},{10,8},{11,9},{8,1... | collective-permute-start | bytes 786440 | tf_op jit(solution)/shard_map/ppermute | solution.py:94
  81.6 2.7 %collective-permute-start.2 = (f32[256,256]{1,0:T(8,128)S(1)}, f32[256,256]{1,0:T(8,128)}, u32[]{:S(2)}, u32[]{:S(2)}) collective-permute-start(f32[256,256]{1,0:T(8,128)S(1)} %get-tuple-element.9.refs_2_), channel_id=1, source_target_pairs={{1,0},{2,1},{3,2},{0,3},{5,4},{6,5},{7,6},{4,7},{9,8},{10,9},{11,1... | collective-permute-start | bytes 786440 | tf_op jit(solution)/shard_map/ppermute | solution.py:94
  84.4 3.5 %all-to-all-done.2.stats_ref = f32[16,8,256]{2,1,0:T(8,128)S(1)} async-done(((f32[16,8,256]{2,1,0:T(8,128)}), f32[16,8,256]{2,1,0:T(8,128)S(1)}, u32[]{:S(2)}, u32[]{:S(2)}) %all-to-all-start.2) | async-done | bytes 131104 | tf_op jit(solution)/shard_map/all_to_all | solution.py:316
  87.8 0.7 merged_stats.1
  88.6 3.5 %all-to-all-start.3 = ((f32[16,8,256]{2,1,0:T(8,128)}), f32[16,8,256]{2,1,0:T(8,128)S(1)}, u32[]{:S(2)}, u32[]{:S(2)}) async-start(f32[16,8,256]{2,1,0:T(8,128)} %merged_stats.1), calls=%async_computation.3 | async-start | bytes 262144 | tf_op jit(solution)/shard_map/all_to_all | solution.py:318
  92.2 7.9 %all-to-all-done.3.refs_0_.stats_ref = f32[16,8,256]{2,1,0:T(8,128)S(1)} async-done(((f32[16,8,256]{2,1,0:T(8,128)}), f32[16,8,256]{2,1,0:T(8,128)S(1)}, u32[]{:S(2)}, u32[]{:S(2)}) %all-to-all-start.3) | async-done | bytes 131104 | tf_op jit(solution)/shard_map/all_to_all | solution.py:318
  100.1 2.8 %partial_grad.1 = bf16[256,1792]{1,0:T(8,128)(2,1)S(1)} custom-call(f32[16,8,256]{2,1,0:T(8,128)S(1)} %all-to-all-done.3.refs_0_.stats_ref, f32[8,256]{1,0:T(8,128)S(1)} %row_meta.1.refs_1_.meta_ref, f32[256,256]{1,0:T(8,128)S(1)} %get-tuple-element.9.refs_2_, f32[256,256]{1,0:T(8,128)} %collective-permute-done.2.refs_3_, ...), custom_call_target="tpu_custom_call" | custom-call | flops 939524096 | bytes 1048576 | tf_op jit(solution)/shard_map/partial_grad/pallas_call | solution.py:274
  102.9 12.6 %all_to_all.31 = bf16[4,64,1792]{2,1,0:T(8,128)(2,1)S(1)} all-to-all(bf16[4,64,1792]{2,1,0:T(8,128)(2,1)S(1)} %bitcast.2), channel_id=1, replica_groups=mesh['y'=4,'c'=2,'z'=16,'x'=4] {'y'}, dimensions={0} | all-to-all | bytes 1835008 | tf_op jit(solution)/shard_map/all_to_all | solution.py:321
  115.5 0.2 reduce_sum.24
  115.7 0.8 reshape.20
  116.4 10.2 %all-to-all-start.5 = ((bf16[16,4,1792]{2,1,0:T(4,128)(2,1)}), bf16[16,4,1792]{2,1,0:T(4,128)(2,1)S(1)}, u32[]{:S(2)}, u32[]{:S(2)}) async-start(bf16[16,4,1792]{2,1,0:T(4,128)(2,1)} %reshape.20), calls=%async_computation.5 | async-start | bytes 458752 | tf_op jit(solution)/shard_map/all_to_all | solution.py:323
  126.6 0.7 rows_loss.1
  127.3 1.9 %collective-permute-start.5 = (f32[]{:T(128)}, f32[]{:T(128)}, u32[]{:S(2)}, u32[]{:S(2)}) collective-permute-start(f32[]{:T(128)} %bitcast.1), channel_id=1, source_target_pairs={{0,64},{64,0},{1,65},{65,1},{2,66},{66,2},{3,67},{67,3},{4,68},{68... | collective-permute-start | bytes 20 | tf_op jit(solution)/shard_map/ppermute | solution.py:326
  129.2 1.2 collective-permute-done.5
  131.7 9.1 %all-to-all-done.5 = bf16[16,4,1792]{2,1,0:T(4,128)(2,1)S(1)} async-done(((bf16[16,4,1792]{2,1,0:T(4,128)(2,1)}), bf16[16,4,1792]{2,1,0:T(4,128)(2,1)S(1)}, u32[]{:S(2)}, u32[]{:S(2)}) %all-to-all-start.5) | async-done | bytes 229408 | tf_op jit(solution)/shard_map/all_to_all | solution.py:323
  140.8 0.7 reduce_sum.25
  (19 shorter events, 0.1 us)
Async XLA Ops:
  2.1 32.1 %all-to-all-start = ((bf16[16,4,1792]{2,1,0:T(4,128)(2,1)}), bf16[16,4,1792]{2,1,0:T(4,128)(2,1)S(1)}, u32[]{:S(2)}, u32[]{:S(2)}) async-start(bf16[16,4,1792]{2,1,0:T(4,128)(2,1)} %broadcast_in_dim.2), calls=%async_computation | async-start | bytes 458752 | tf_op jit(solution)/shard_map/all_to_all | solution.py:90
  17.3 7.4 %copy-start.5 = (s32[512]{0:T(512)S(1)}, s32[512]{0:T(512)}, u32[]{:S(2)}) copy-start(s32[512]{0:T(512)} %param.9) | copy-start | bytes 6148
  17.3 7.6 %copy-start.1 = (s32[32]{0:T(128)S(1)}, s32[32]{0:T(128)}, u32[]{:S(2)}) copy-start(s32[32]{0:T(128)} %offsets.1) | copy-start | bytes 388
  17.3 7.6 %copy-start.2 = (s32[32]{0:T(128)S(1)}, s32[32]{0:T(128)}, u32[]{:S(2)}) copy-start(s32[32]{0:T(128)} %lengths.1) | copy-start | bytes 388
  17.4 7.6 %copy-start.3 = (s32[32]{0:T(128)S(1)}, s32[32]{0:T(128)}, u32[]{:S(2)}) copy-start(s32[32]{0:T(128)} %groups.1) | copy-start | bytes 388
  17.4 7.5 %copy-start.4 = (f32[32]{0:T(128)S(1)}, f32[32]{0:T(128)}, u32[]{:S(2)}) copy-start(f32[32]{0:T(128)} %rewards.1) | copy-start | bytes 388
  17.4 31.4 %copy-start = (bf16[1792,512]{1,0:T(8,128)(2,1)S(1)}, bf16[1792,512]{1,0:T(8,128)(2,1)}, u32[]{:S(2)}) copy-start(bf16[1792,512]{1,0:T(8,128)(2,1)} %refs_6_.1) | copy-start | bytes 5505028
  20.4 28.4 %collective-permute-start.1 = (bf16[896,512]{1,0:T(8,128)(2,1)}, bf16[896,512]{1,0:T(8,128)(2,1)S(1)}, u32[]{:S(2)}, u32[]{:S(2)}) collective-permute-start(bf16[896,512]{1,0:T(8,128)(2,1)} %get-tuple-element.10), channel_id=1, source_target_pairs={{0,64},{64,0},{1,65},{65,1},{2,66},{66,2},{3,67},{67,3},{4,68},{68... | collective-permute-start | bytes 2752520 | tf_op jit(solution)/shard_map/ppermute | solution.py:309
  22.3 26.5 %collective-permute-start = (bf16[896,512]{1,0:T(8,128)(2,1)}, bf16[896,512]{1,0:T(8,128)(2,1)}, u32[]{:S(2)}, u32[]{:S(2)}) collective-permute-start(bf16[896,512]{1,0:T(8,128)(2,1)} %get-tuple-element.11), channel_id=1, source_target_pairs={{0,64},{64,0},{1,65},{65,1},{2,66},{66,2},{3,67},{67,3},{4,68},{68... | collective-permute-start | bytes 2752520 | tf_op jit(solution)/shard_map/ppermute | solution.py:309
  69.0 18.8 %all-to-all-start.2 = ((f32[16,8,256]{2,1,0:T(8,128)}), f32[16,8,256]{2,1,0:T(8,128)S(1)}, u32[]{:S(2)}, u32[]{:S(2)}) async-start(f32[16,8,256]{2,1,0:T(8,128)} %get-tuple-element.8), calls=%async_computation.2 | async-start | bytes 262144 | tf_op jit(solution)/shard_map/all_to_all | solution.py:316
  75.2 16.9 %collective-permute-start.4 = (f32[256,256]{1,0:T(8,128)S(1)}, f32[256,256]{1,0:T(8,128)S(1)}, u32[]{:S(2)}, u32[]{:S(2)}) collective-permute-start(f32[256,256]{1,0:T(8,128)S(1)} %get-tuple-element.9.refs_2_), channel_id=1, source_target_pairs={{3,0},{0,1},{1,2},{2,3},{7,4},{4,5},{5,6},{6,7},{11,8},{8,9},{9,10... | collective-permute-start | bytes 786440 | tf_op jit(solution)/shard_map/ppermute | solution.py:94
  77.7 14.4 %collective-permute-start.3 = (f32[256,256]{1,0:T(8,128)S(1)}, f32[256,256]{1,0:T(8,128)}, u32[]{:S(2)}, u32[]{:S(2)}) collective-permute-start(f32[256,256]{1,0:T(8,128)S(1)} %get-tuple-element.9.refs_2_), channel_id=1, source_target_pairs={{2,0},{3,1},{0,2},{1,3},{6,4},{7,5},{4,6},{5,7},{10,8},{11,9},{8,1... | collective-permute-start | bytes 786440 | tf_op jit(solution)/shard_map/ppermute | solution.py:94
  81.6 10.5 %collective-permute-start.2 = (f32[256,256]{1,0:T(8,128)S(1)}, f32[256,256]{1,0:T(8,128)}, u32[]{:S(2)}, u32[]{:S(2)}) collective-permute-start(f32[256,256]{1,0:T(8,128)S(1)} %get-tuple-element.9.refs_2_), channel_id=1, source_target_pairs={{1,0},{2,1},{3,2},{0,3},{5,4},{6,5},{7,6},{4,7},{9,8},{10,9},{11,1... | collective-permute-start | bytes 786440 | tf_op jit(solution)/shard_map/ppermute | solution.py:94
  88.6 11.5 %all-to-all-start.3 = ((f32[16,8,256]{2,1,0:T(8,128)}), f32[16,8,256]{2,1,0:T(8,128)S(1)}, u32[]{:S(2)}, u32[]{:S(2)}) async-start(f32[16,8,256]{2,1,0:T(8,128)} %merged_stats.1), calls=%async_computation.3 | async-start | bytes 262144 | tf_op jit(solution)/shard_map/all_to_all | solution.py:318
  116.4 24.4 %all-to-all-start.5 = ((bf16[16,4,1792]{2,1,0:T(4,128)(2,1)}), bf16[16,4,1792]{2,1,0:T(4,128)(2,1)S(1)}, u32[]{:S(2)}, u32[]{:S(2)}) async-start(bf16[16,4,1792]{2,1,0:T(4,128)(2,1)} %reshape.20), calls=%async_computation.5 | async-start | bytes 458752 | tf_op jit(solution)/shard_map/all_to_all | solution.py:323
  127.3 3.1 %collective-permute-start.5 = (f32[]{:T(128)}, f32[]{:T(128)}, u32[]{:S(2)}, u32[]{:S(2)}) collective-permute-start(f32[]{:T(128)} %bitcast.1), channel_id=1, source_target_pairs={{0,64},{64,0},{1,65},{65,1},{2,66},{66,2},{3,67},{67,3},{4,68},{68... | collective-permute-start | bytes 20 | tf_op jit(solution)/shard_map/ppermute | solution.py:326

commit v5 on v4

--- a/solution.py
+++ b/solution.py
@@ -67,9 +67,17 @@
     )
 
 
+def fold(rows):
+    half = rows.shape[1] // 2
+    return jnp.concatenate([rows[:, :half], rows[:, half:]], axis=0)
+
+
+def unfolded(stats_ref):
+    return [jnp.concatenate([stats_ref[:, i], stats_ref[:, 4 + i]], axis=1) for i in range(4)]
+
+
 def merge_kernel(stats_ref, out_ref):
-    parts = merge(*(stats_ref[:, i] for i in range(4)))
-    block = jnp.concatenate([*parts, *parts], axis=0)
+    block = fold(jnp.concatenate(merge(*unfolded(stats_ref)), axis=0))
     for i in range(out_ref.shape[0]):
         out_ref[i] = block
 
@@ -176,7 +184,7 @@
     packed = jnp.zeros((n, 128), jnp.float32)
     for i, value in enumerate(values):
         packed = jnp.where(lane == i, value, packed)
-    packed = packed.T[:8]
+    packed = fold(packed.T[:4])
     for i in range(Z):
         stats_ref[i] = packed
 
@@ -187,7 +195,7 @@
         lambda *refs: stats_kernel(vocab, *refs),
         out_shape=(
             jax.ShapeDtypeStruct((n, width), jnp.float32),
-            jax.ShapeDtypeStruct((Z, 8, n), jnp.float32),
+            jax.ShapeDtypeStruct((Z, 8, n // 2), jnp.float32),
         ),
         in_specs=[VMEM, VMEM],
         out_specs=(VMEM, VMEM),
@@ -200,7 +208,7 @@
 
 
 def row_terms(stats_ref):
-    top, total, weighted, target = merge(*(stats_ref[:, i] for i in range(4)))
+    top, total, weighted, target = merge(*unfolded(stats_ref))
     log_sum = jnp.log(total)
     return top + log_sum, log_sum - weighted / total, target
 

time: 144 us -> 143 us (level)
  transfers between devices with their start and end apart: 10 -> 10, of which waited for: 6 -> 6; matrix products, arithmetic and copies ran while one was open for 2% -> 2% of each run, Pallas kernels for 2% -> 1%
where the time goes in v5:
time: 143 us; the launch traced here: 142 us
  starting transfers between devices  51.3 us (36%)
  blocking collectives  44.4 us (31%)
  waiting for transfers between devices  29.2 us (20%)
  Pallas kernels  7.81 us (5%)
  local copies, waits for them, and re-layouts  5.49 us (4%)
  between operations  3.27 us (2%)
    all_to_all x1, blocking collectives, per_device(): part = lax.all_to_all(part, 'x', 0, 0, tiled=True)  17.3 us
    all_to_all x1, starting transfers between devices, spread(): return lax.all_to_all(sent, axes, 0, 0, tiled=True)  15.2 us
    all_gather x1, blocking collectives, per_device(): my_rows = lax.all_gather(tok_rows, 'y', axis=0, tiled=True)  14.5 us
    all_to_all x1, blocking collectives, per_device(): lax.all_to_all(hidden_grad.reshape(Y, per_tok, depth), 'y', 0, 0, tiled=T...  12.6 us
    all_to_all x1, starting transfers between devices, per_device(): lax.all_to_all(hidden_grad.reshape(Z, per_tok // Z, depth), 'z', 0, 0, ti...  11 us
    ppermute x3, starting transfers between devices, x_neighbour(): return lax.ppermute(block, 'x', [((i + k) % X, i) for i in range(X)])  9.17 us
    all_to_all x1, waiting for transfers between devices, per_device(): lax.all_to_all(hidden_grad.reshape(Z, per_tok // Z, depth), 'z', 0, 0, ti...  9.13 us
    all_to_all x1, waiting for transfers between devices, spread(): return lax.all_to_all(sent, axes, 0, 0, tiled=True)  8.54 us
  transfers between devices with their start and end apart: 10, of which 6 were waited for; matrix products, arithmetic and copies ran while one was open for 2% of the time, Pallas kernels for 1%

profile of v5, /device:TPU:32, one launch (start us, length us, event | category | flops | bytes accessed | tf_op | source)
XLA Modules:
  0.0 142.3 jit_solution(17116938229972320296)
XLA Ops:
  0.6 1.5 %broadcast_in_dim.2 = bf16[16,4,1792]{2,1,0:T(4,128)(2,1)} broadcast(bf16[4,1792]{1,0:T(4,128)(2,1)} %param.7), dimensions={1,2} | broadcast | bytes 243712 | tf_op jit(solution)/shard_map/broadcast_in_dim | solution.py:97
  2.1 15.2 %all-to-all-start = ((bf16[16,4,1792]{2,1,0:T(4,128)(2,1)}), bf16[16,4,1792]{2,1,0:T(4,128)(2,1)S(1)}, u32[]{:S(2)}, u32[]{:S(2)}) async-start(bf16[16,4,1792]{2,1,0:T(4,128)(2,1)} %broadcast_in_dim.2), calls=%async_computation | async-start | bytes 458752 | tf_op jit(solution)/shard_map/all_to_all | solution.py:98
  17.4 3.0 %fusion = (bf16[896,512]{1,0:T(8,128)(2,1)}, bf16[896,512]{1,0:T(8,128)(2,1)}) fusion(bf16[1792,512]{1,0:T(8,128)(2,1)} %refs_6_.1), kind=kLoop, calls=%fused_computation.1 | loop fusion | bytes 3670016 | tf_op jit(solution)/shard_map/split | solution.py:317
  20.4 1.9 %collective-permute-start.1 = (bf16[896,512]{1,0:T(8,128)(2,1)}, bf16[896,512]{1,0:T(8,128)(2,1)S(1)}, u32[]{:S(2)}, u32[]{:S(2)}) collective-permute-start(bf16[896,512]{1,0:T(8,128)(2,1)} %get-tuple-element.10), channel_id=1, source_target_pairs={{0,64},{64,0},{1,65},{65,1},{2,66},{66,2},{3,67},{67,3},{4,68},{68... | collective-permute-start | bytes 2752520 | tf_op jit(solution)/shard_map/ppermute | solution.py:317
  22.3 2.4 %collective-permute-start = (bf16[896,512]{1,0:T(8,128)(2,1)}, bf16[896,512]{1,0:T(8,128)(2,1)}, u32[]{:S(2)}, u32[]{:S(2)}) collective-permute-start(bf16[896,512]{1,0:T(8,128)(2,1)} %get-tuple-element.11), channel_id=1, source_target_pairs={{0,64},{64,0},{1,65},{65,1},{2,66},{66,2},{3,67},{67,3},{4,68},{68... | collective-permute-start | bytes 2752520 | tf_op jit(solution)/shard_map/ppermute | solution.py:317
  24.7 0.1 reshape.18
  24.8 0.1 reshape_squeeze.3.target_ref
  24.9 0.8 row_meta.1.refs_1_.meta_ref
  25.7 8.5 %all-to-all-done = bf16[16,4,1792]{2,1,0:T(4,128)(2,1)S(1)} async-done(((bf16[16,4,1792]{2,1,0:T(4,128)(2,1)}), bf16[16,4,1792]{2,1,0:T(4,128)(2,1)S(1)}, u32[]{:S(2)}, u32[]{:S(2)}) %all-to-all-start) | async-done | bytes 229408 | tf_op jit(solution)/shard_map/all_to_all | solution.py:98
  34.3 14.5 %all_gather.3.rows_ref = bf16[256,1792]{1,0:T(8,128)(2,1)S(1)} all-gather(bf16[64,1792]{1,0:T(8,128)(2,1)S(1)} %reshape.17), channel_id=1, replica_groups=mesh['y'=4,'c'=2,'z'=16,'x'=4] {'y'}, dimensions={0}, use_global_device_ids=true | all-gather | bytes 1146880 | tf_op jit(solution)/shard_map/all_gather | solution.py:319
  48.8 1.8 %partial_logits.1 = f32[4,256,256]{2,1,0:T(8,128)S(1)} custom-call(bf16[256,1792]{1,0:T(8,128)(2,1)S(1)} %all_gather.3.rows_ref, bf16[1792,512]{1,0:T(8,128)(2,1)S(1)} %copy-done, bf16[896,512]{1,0:T(8,128)(2,1)} %collective-permute-done.refs_0_.refs_7_, bf16[896,512]{1,0:T(8,128)(2,1)S(1)} %collective-permute-done.1.refs_1_.refs_8_), custom_call_target="tpu_custom_call" | custom-call | flops 939524096 | bytes 1048576 | tf_op jit(solution)/shard_map/partial_logits/pallas_call | solution.py:144
  50.6 17.3 %all_to_all.30.refs_0_ = f32[4,256,256]{2,1,0:T(8,128)S(1)} all-to-all(f32[4,256,256]{2,1,0:T(8,128)S(1)} %partial_logits.1), channel_id=1, replica_groups=mesh['y'=4,'c'=2,'z'=16,'x'=4] {'x'}, dimensions={0} | all-to-all | bytes 2097152 | tf_op jit(solution)/shard_map/all_to_all | solution.py:322
  67.9 1.0 local_stats.1
  69.0 6.2 %all-to-all-start.2 = ((f32[16,8,128]{2,1,0:T(8,128)}), f32[16,8,128]{2,1,0:T(8,128)S(1)}, u32[]{:S(2)}, u32[]{:S(2)}) async-start(f32[16,8,128]{2,1,0:T(8,128)} %get-tuple-element.8), calls=%async_computation.2 | async-start | bytes 131072 | tf_op jit(solution)/shard_map/all_to_all | solution.py:324
  75.2 2.5 %collective-permute-start.4 = (f32[256,256]{1,0:T(8,128)S(1)}, f32[256,256]{1,0:T(8,128)S(1)}, u32[]{:S(2)}, u32[]{:S(2)}) collective-permute-start(f32[256,256]{1,0:T(8,128)S(1)} %get-tuple-element.9.refs_2_), channel_id=1, source_target_pairs={{3,0},{0,1},{1,2},{2,3},{7,4},{4,5},{5,6},{6,7},{11,8},{8,9},{9,10... | collective-permute-start | bytes 786440 | tf_op jit(solution)/shard_map/ppermute | solution.py:102
  77.6 4.0 %collective-permute-start.3 = (f32[256,256]{1,0:T(8,128)S(1)}, f32[256,256]{1,0:T(8,128)}, u32[]{:S(2)}, u32[]{:S(2)}) collective-permute-start(f32[256,256]{1,0:T(8,128)S(1)} %get-tuple-element.9.refs_2_), channel_id=1, source_target_pairs={{2,0},{3,1},{0,2},{1,3},{6,4},{7,5},{4,6},{5,7},{10,8},{11,9},{8,1... | collective-permute-start | bytes 786440 | tf_op jit(solution)/shard_map/ppermute | solution.py:102
  81.6 2.7 %collective-permute-start.2 = (f32[256,256]{1,0:T(8,128)S(1)}, f32[256,256]{1,0:T(8,128)}, u32[]{:S(2)}, u32[]{:S(2)}) collective-permute-start(f32[256,256]{1,0:T(8,128)S(1)} %get-tuple-element.9.refs_2_), channel_id=1, source_target_pairs={{1,0},{2,1},{3,2},{0,3},{5,4},{6,5},{7,6},{4,7},{9,8},{10,9},{11,1... | collective-permute-start | bytes 786440 | tf_op jit(solution)/shard_map/ppermute | solution.py:102
  84.4 2.6 %all-to-all-done.2.stats_ref = f32[16,8,128]{2,1,0:T(8,128)S(1)} async-done(((f32[16,8,128]{2,1,0:T(8,128)}), f32[16,8,128]{2,1,0:T(8,128)S(1)}, u32[]{:S(2)}, u32[]{:S(2)}) %all-to-all-start.2) | async-done | bytes 65568 | tf_op jit(solution)/shard_map/all_to_all | solution.py:324
  87.0 0.7 merged_stats.1
  87.7 3.6 %all-to-all-start.3 = ((f32[16,8,128]{2,1,0:T(8,128)}), f32[16,8,128]{2,1,0:T(8,128)S(1)}, u32[]{:S(2)}, u32[]{:S(2)}) async-start(f32[16,8,128]{2,1,0:T(8,128)} %merged_stats.1), calls=%async_computation.3 | async-start | bytes 131072 | tf_op jit(solution)/shard_map/all_to_all | solution.py:326
  91.3 0.5 collective-permute-done.2.refs_3_
  91.8 7.1 %all-to-all-done.3.refs_0_.stats_ref = f32[16,8,128]{2,1,0:T(8,128)S(1)} async-done(((f32[16,8,128]{2,1,0:T(8,128)}), f32[16,8,128]{2,1,0:T(8,128)S(1)}, u32[]{:S(2)}, u32[]{:S(2)}) %all-to-all-start.3) | async-done | bytes 65568 | tf_op jit(solution)/shard_map/all_to_all | solution.py:326
  98.9 2.8 %partial_grad.1 = bf16[256,1792]{1,0:T(8,128)(2,1)S(1)} custom-call(f32[16,8,128]{2,1,0:T(8,128)S(1)} %all-to-all-done.3.refs_0_.stats_ref, f32[8,256]{1,0:T(8,128)S(1)} %row_meta.1.refs_1_.meta_ref, f32[256,256]{1,0:T(8,128)S(1)} %get-tuple-element.9.refs_2_, f32[256,256]{1,0:T(8,128)} %collective-permute-done.2.refs_3_, ...), custom_call_target="tpu_custom_call" | custom-call | flops 939524096 | bytes 1048576 | tf_op jit(solution)/shard_map/partial_grad/pallas_call | solution.py:282
  101.8 12.6 %all_to_all.31 = bf16[4,64,1792]{2,1,0:T(8,128)(2,1)S(1)} all-to-all(bf16[4,64,1792]{2,1,0:T(8,128)(2,1)S(1)} %bitcast.2), channel_id=1, replica_groups=mesh['y'=4,'c'=2,'z'=16,'x'=4] {'y'}, dimensions={0} | all-to-all | bytes 1835008 | tf_op jit(solution)/shard_map/all_to_all | solution.py:329
  114.4 0.2 reduce_sum.24
  114.5 0.8 reshape.20
  115.3 11.0 %all-to-all-start.5 = ((bf16[16,4,1792]{2,1,0:T(4,128)(2,1)}), bf16[16,4,1792]{2,1,0:T(4,128)(2,1)S(1)}, u32[]{:S(2)}, u32[]{:S(2)}) async-start(bf16[16,4,1792]{2,1,0:T(4,128)(2,1)} %reshape.20), calls=%async_computation.5 | async-start | bytes 458752 | tf_op jit(solution)/shard_map/all_to_all | solution.py:331
  126.2 0.7 rows_loss.1
  126.9 1.9 %collective-permute-start.5 = (f32[]{:T(128)}, f32[]{:T(128)}, u32[]{:S(2)}, u32[]{:S(2)}) collective-permute-start(f32[]{:T(128)} %bitcast.1), channel_id=1, source_target_pairs={{0,64},{64,0},{1,65},{65,1},{2,66},{66,2},{3,67},{67,3},{4,68},{68... | collective-permute-start | bytes 20 | tf_op jit(solution)/shard_map/ppermute | solution.py:334
  128.8 1.2 collective-permute-done.5
  131.3 9.1 %all-to-all-done.5 = bf16[16,4,1792]{2,1,0:T(4,128)(2,1)S(1)} async-done(((bf16[16,4,1792]{2,1,0:T(4,128)(2,1)}), bf16[16,4,1792]{2,1,0:T(4,128)(2,1)S(1)}, u32[]{:S(2)}, u32[]{:S(2)}) %all-to-all-start.5) | async-done | bytes 229408 | tf_op jit(solution)/shard_map/all_to_all | solution.py:331
  140.5 0.7 reduce_sum.25
  (19 shorter events, 0.1 us)
Async XLA Ops:
  2.1 32.1 %all-to-all-start = ((bf16[16,4,1792]{2,1,0:T(4,128)(2,1)}), bf16[16,4,1792]{2,1,0:T(4,128)(2,1)S(1)}, u32[]{:S(2)}, u32[]{:S(2)}) async-start(bf16[16,4,1792]{2,1,0:T(4,128)(2,1)} %broadcast_in_dim.2), calls=%async_computation | async-start | bytes 458752 | tf_op jit(solution)/shard_map/all_to_all | solution.py:98
  17.3 7.4 %copy-start.5 = (s32[512]{0:T(512)S(1)}, s32[512]{0:T(512)}, u32[]{:S(2)}) copy-start(s32[512]{0:T(512)} %param.9) | copy-start | bytes 6148
  17.3 7.6 %copy-start.1 = (s32[32]{0:T(128)S(1)}, s32[32]{0:T(128)}, u32[]{:S(2)}) copy-start(s32[32]{0:T(128)} %offsets.1) | copy-start | bytes 388
  17.3 7.6 %copy-start.2 = (s32[32]{0:T(128)S(1)}, s32[32]{0:T(128)}, u32[]{:S(2)}) copy-start(s32[32]{0:T(128)} %lengths.1) | copy-start | bytes 388
  17.4 7.6 %copy-start.3 = (s32[32]{0:T(128)S(1)}, s32[32]{0:T(128)}, u32[]{:S(2)}) copy-start(s32[32]{0:T(128)} %groups.1) | copy-start | bytes 388
  17.4 7.5 %copy-start.4 = (f32[32]{0:T(128)S(1)}, f32[32]{0:T(128)}, u32[]{:S(2)}) copy-start(f32[32]{0:T(128)} %rewards.1) | copy-start | bytes 388
  17.4 31.4 %copy-start = (bf16[1792,512]{1,0:T(8,128)(2,1)S(1)}, bf16[1792,512]{1,0:T(8,128)(2,1)}, u32[]{:S(2)}) copy-start(bf16[1792,512]{1,0:T(8,128)(2,1)} %refs_6_.1) | copy-start | bytes 5505028
  20.4 28.4 %collective-permute-start.1 = (bf16[896,512]{1,0:T(8,128)(2,1)}, bf16[896,512]{1,0:T(8,128)(2,1)S(1)}, u32[]{:S(2)}, u32[]{:S(2)}) collective-permute-start(bf16[896,512]{1,0:T(8,128)(2,1)} %get-tuple-element.10), channel_id=1, source_target_pairs={{0,64},{64,0},{1,65},{65,1},{2,66},{66,2},{3,67},{67,3},{4,68},{68... | collective-permute-start | bytes 2752520 | tf_op jit(solution)/shard_map/ppermute | solution.py:317
  22.3 26.5 %collective-permute-start = (bf16[896,512]{1,0:T(8,128)(2,1)}, bf16[896,512]{1,0:T(8,128)(2,1)}, u32[]{:S(2)}, u32[]{:S(2)}) collective-permute-start(bf16[896,512]{1,0:T(8,128)(2,1)} %get-tuple-element.11), channel_id=1, source_target_pairs={{0,64},{64,0},{1,65},{65,1},{2,66},{66,2},{3,67},{67,3},{4,68},{68... | collective-permute-start | bytes 2752520 | tf_op jit(solution)/shard_map/ppermute | solution.py:317
  69.0 18.0 %all-to-all-start.2 = ((f32[16,8,128]{2,1,0:T(8,128)}), f32[16,8,128]{2,1,0:T(8,128)S(1)}, u32[]{:S(2)}, u32[]{:S(2)}) async-start(f32[16,8,128]{2,1,0:T(8,128)} %get-tuple-element.8), calls=%async_computation.2 | async-start | bytes 131072 | tf_op jit(solution)/shard_map/all_to_all | solution.py:324
  75.2 16.1 %collective-permute-start.4 = (f32[256,256]{1,0:T(8,128)S(1)}, f32[256,256]{1,0:T(8,128)S(1)}, u32[]{:S(2)}, u32[]{:S(2)}) collective-permute-start(f32[256,256]{1,0:T(8,128)S(1)} %get-tuple-element.9.refs_2_), channel_id=1, source_target_pairs={{3,0},{0,1},{1,2},{2,3},{7,4},{4,5},{5,6},{6,7},{11,8},{8,9},{9,10... | collective-permute-start | bytes 786440 | tf_op jit(solution)/shard_map/ppermute | solution.py:102
  77.6 13.6 %collective-permute-start.3 = (f32[256,256]{1,0:T(8,128)S(1)}, f32[256,256]{1,0:T(8,128)}, u32[]{:S(2)}, u32[]{:S(2)}) collective-permute-start(f32[256,256]{1,0:T(8,128)S(1)} %get-tuple-element.9.refs_2_), channel_id=1, source_target_pairs={{2,0},{3,1},{0,2},{1,3},{6,4},{7,5},{4,6},{5,7},{10,8},{11,9},{8,1... | collective-permute-start | bytes 786440 | tf_op jit(solution)/shard_map/ppermute | solution.py:102
  81.6 10.2 %collective-permute-start.2 = (f32[256,256]{1,0:T(8,128)S(1)}, f32[256,256]{1,0:T(8,128)}, u32[]{:S(2)}, u32[]{:S(2)}) collective-permute-start(f32[256,256]{1,0:T(8,128)S(1)} %get-tuple-element.9.refs_2_), channel_id=1, source_target_pairs={{1,0},{2,1},{3,2},{0,3},{5,4},{6,5},{7,6},{4,7},{9,8},{10,9},{11,1... | collective-permute-start | bytes 786440 | tf_op jit(solution)/shard_map/ppermute | solution.py:102
  87.7 11.3 %all-to-all-start.3 = ((f32[16,8,128]{2,1,0:T(8,128)}), f32[16,8,128]{2,1,0:T(8,128)S(1)}, u32[]{:S(2)}, u32[]{:S(2)}) async-start(f32[16,8,128]{2,1,0:T(8,128)} %merged_stats.1), calls=%async_computation.3 | async-start | bytes 131072 | tf_op jit(solution)/shard_map/all_to_all | solution.py:326
  115.3 25.2 %all-to-all-start.5 = ((bf16[16,4,1792]{2,1,0:T(4,128)(2,1)}), bf16[16,4,1792]{2,1,0:T(4,128)(2,1)S(1)}, u32[]{:S(2)}, u32[]{:S(2)}) async-start(bf16[16,4,1792]{2,1,0:T(4,128)(2,1)} %reshape.20), calls=%async_computation.5 | async-start | bytes 458752 | tf_op jit(solution)/shard_map/all_to_all | solution.py:331
  126.9 3.1 %collective-permute-start.5 = (f32[]{:T(128)}, f32[]{:T(128)}, u32[]{:S(2)}, u32[]{:S(2)}) collective-permute-start(f32[]{:T(128)} %bitcast.1), channel_id=1, source_target_pairs={{0,64},{64,0},{1,65},{65,1},{2,66},{66,2},{3,67},{67,3},{4,68},{68... | collective-permute-start | bytes 20 | tf_op jit(solution)/shard_map/ppermute | solution.py:334

commit v6 on v5

--- a/solution.py
+++ b/solution.py
@@ -185,7 +185,7 @@
     for i, value in enumerate(values):
         packed = jnp.where(lane == i, value, packed)
     packed = fold(packed.T[:4])
-    for i in range(Z):
+    for i in range(stats_ref.shape[0]):
         stats_ref[i] = packed
 
 
@@ -195,7 +195,7 @@
         lambda *refs: stats_kernel(vocab, *refs),
         out_shape=(
             jax.ShapeDtypeStruct((n, width), jnp.float32),
-            jax.ShapeDtypeStruct((Z, 8, n // 2), jnp.float32),
+            jax.ShapeDtypeStruct((Y * X, 8, n // 2), jnp.float32),
         ),
         in_specs=[VMEM, VMEM],
         out_specs=(VMEM, VMEM),
@@ -321,9 +321,9 @@
     part = partial_logits(my_rows, head_weight, other_weight)
     part = lax.all_to_all(part, "x", 0, 0, tiled=True)
     logits, stats = local_stats(part, meta, vocab)
-    stats = lax.all_to_all(stats, "z", 0, 0, tiled=True)
+    stats = lax.all_to_all(stats, ("y", "x"), 0, 0, tiled=True)
     chunks = [logits, *(x_neighbour(logits, k) for k in range(1, X))]
-    stats = lax.all_to_all(merged_stats(stats, Y * X), ("y", "x"), 0, 0, tiled=True)
+    stats = lax.all_to_all(merged_stats(stats, Z), "z", 0, 0, tiled=True)
     hidden_grad = partial_grad(stats, meta, chunks, head_weight, other_weight)
 
     hidden_grad = lax.all_to_all(hidden_grad.reshape(Y, per_tok, depth), "y", 0, 0, tiled=True)

time: 143 us -> 142 us (level)
  starting transfers between devices: 51.3 us -> 47.4 us
  blocking collectives: 44.4 us -> 46 us
  waiting for transfers between devices: 29.2 us -> 30.8 us
    all_to_all x1, starting transfers between devices: 11 us -> 4.42 us  [per_device(): lax.all_to_all(hidden_grad.reshape(Z, per_tok // Z, depth), 'z', 0, 0, ti...]
    ppermute x3, starting transfers between devices: 9.17 us -> 11.8 us  [x_neighbour(): return lax.ppermute(block, 'x', [((i + k) % X, i) for i in range(X)])]
    all_to_all x2, waiting for transfers between devices: 9.78 us -> 11.8 us  [the longest x1 11.8 us: per_device(): stats = lax.all_to_all(merged_stats(stats, Z), 'z', 0, 0, tiled=True)]
    all_to_all x1, blocking collectives: 12.6 us -> 14.2 us  [per_device(): lax.all_to_all(hidden_grad.reshape(Y, per_tok, depth), 'y', 0, 0, tiled=T...]
  transfers between devices with their start and end apart: 10 -> 10, of which waited for: 6 -> 4; matrix products, arithmetic and copies ran while one was open for 2% -> 2% of each run, Pallas kernels for 1% -> 1%
where the time goes in v6:
time: 142 us
  starting transfers between devices  47.4 us (33%)
  blocking collectives  46 us (32%)
  waiting for transfers between devices  30.8 us (22%)
  Pallas kernels  7.81 us (6%)
  local copies, waits for them, and re-layouts  5.49 us (4%)
  between operations  3.28 us (2%)
    all_to_all x1, blocking collectives, per_device(): part = lax.all_to_all(part, 'x', 0, 0, tiled=True)  17.3 us
    all_to_all x1, starting transfers between devices, spread(): return lax.all_to_all(sent, axes, 0, 0, tiled=True)  15.2 us
    all_gather x1, blocking collectives, per_device(): my_rows = lax.all_gather(tok_rows, 'y', axis=0, tiled=True)  14.5 us
    all_to_all x1, blocking collectives, per_device(): lax.all_to_all(hidden_grad.reshape(Y, per_tok, depth), 'y', 0, 0, tiled=T...  14.2 us
    all_to_all x1, waiting for transfers between devices, per_device(): stats = lax.all_to_all(merged_stats(stats, Z), 'z', 0, 0, tiled=True)  11.8 us
    ppermute x3, starting transfers between devices, x_neighbour(): return lax.ppermute(block, 'x', [((i + k) % X, i) for i in range(X)])  11.8 us
    all_to_all x1, waiting for transfers between devices, per_device(): lax.all_to_all(hidden_grad.reshape(Z, per_tok // Z, depth), 'z', 0, 0, ti...  9.23 us
    all_to_all x1, waiting for transfers between devices, spread(): return lax.all_to_all(sent, axes, 0, 0, tiled=True)  8.54 us
  transfers between devices with their start and end apart: 10, of which 4 were waited for; matrix products, arithmetic and copies ran while one was open for 2% of the time, Pallas kernels for 1%

profile of v6, /device:TPU:32, one launch (start us, length us, event | category | flops | bytes accessed | tf_op | source)
XLA Modules:
  0.0 141.6 jit_solution(8832590952669743847)
XLA Ops:
  0.6 1.5 %broadcast_in_dim.2 = bf16[16,4,1792]{2,1,0:T(4,128)(2,1)} broadcast(bf16[4,1792]{1,0:T(4,128)(2,1)} %param.7), dimensions={1,2} | broadcast | bytes 243712 | tf_op jit(solution)/shard_map/broadcast_in_dim | solution.py:97
  2.1 15.2 %all-to-all-start = ((bf16[16,4,1792]{2,1,0:T(4,128)(2,1)}), bf16[16,4,1792]{2,1,0:T(4,128)(2,1)S(1)}, u32[]{:S(2)}, u32[]{:S(2)}) async-start(bf16[16,4,1792]{2,1,0:T(4,128)(2,1)} %broadcast_in_dim.2), calls=%async_computation | async-start | bytes 458752 | tf_op jit(solution)/shard_map/all_to_all | solution.py:98
  17.3 0.0 copy-start.2
  17.4 3.0 %fusion = (bf16[896,512]{1,0:T(8,128)(2,1)}, bf16[896,512]{1,0:T(8,128)(2,1)}) fusion(bf16[1792,512]{1,0:T(8,128)(2,1)} %refs_6_.1), kind=kLoop, calls=%fused_computation.1 | loop fusion | bytes 3670016 | tf_op jit(solution)/shard_map/split | solution.py:317
  20.4 1.9 %collective-permute-start.1 = (bf16[896,512]{1,0:T(8,128)(2,1)}, bf16[896,512]{1,0:T(8,128)(2,1)S(1)}, u32[]{:S(2)}, u32[]{:S(2)}) collective-permute-start(bf16[896,512]{1,0:T(8,128)(2,1)} %get-tuple-element.10), channel_id=1, source_target_pairs={{0,64},{64,0},{1,65},{65,1},{2,66},{66,2},{3,67},{67,3},{4,68},{68... | collective-permute-start | bytes 2752520 | tf_op jit(solution)/shard_map/ppermute | solution.py:317
  22.3 2.4 %collective-permute-start = (bf16[896,512]{1,0:T(8,128)(2,1)}, bf16[896,512]{1,0:T(8,128)(2,1)}, u32[]{:S(2)}, u32[]{:S(2)}) collective-permute-start(bf16[896,512]{1,0:T(8,128)(2,1)} %get-tuple-element.11), channel_id=1, source_target_pairs={{0,64},{64,0},{1,65},{65,1},{2,66},{66,2},{3,67},{67,3},{4,68},{68... | collective-permute-start | bytes 2752520 | tf_op jit(solution)/shard_map/ppermute | solution.py:317
  24.7 0.1 reshape.18
  24.8 0.1 reshape_squeeze.3.target_ref
  24.9 0.8 row_meta.1.refs_1_.meta_ref
  25.7 8.5 %all-to-all-done = bf16[16,4,1792]{2,1,0:T(4,128)(2,1)S(1)} async-done(((bf16[16,4,1792]{2,1,0:T(4,128)(2,1)}), bf16[16,4,1792]{2,1,0:T(4,128)(2,1)S(1)}, u32[]{:S(2)}, u32[]{:S(2)}) %all-to-all-start) | async-done | bytes 229408 | tf_op jit(solution)/shard_map/all_to_all | solution.py:98
  34.2 0.1 reshape.17
  34.3 14.5 %all_gather.3.rows_ref = bf16[256,1792]{1,0:T(8,128)(2,1)S(1)} all-gather(bf16[64,1792]{1,0:T(8,128)(2,1)S(1)} %reshape.17), channel_id=1, replica_groups=mesh['y'=4,'c'=2,'z'=16,'x'=4] {'y'}, dimensions={0}, use_global_device_ids=true | all-gather | bytes 1146880 | tf_op jit(solution)/shard_map/all_gather | solution.py:319
  48.8 1.8 %partial_logits.1 = f32[4,256,256]{2,1,0:T(8,128)S(1)} custom-call(bf16[256,1792]{1,0:T(8,128)(2,1)S(1)} %all_gather.3.rows_ref, bf16[1792,512]{1,0:T(8,128)(2,1)S(1)} %copy-done, bf16[896,512]{1,0:T(8,128)(2,1)} %collective-permute-done.refs_0_.refs_7_, bf16[896,512]{1,0:T(8,128)(2,1)S(1)} %collective-permute-done.1.refs_1_.refs_8_), custom_call_target="tpu_custom_call" | custom-call | flops 939524096 | bytes 1048576 | tf_op jit(solution)/shard_map/partial_logits/pallas_call | solution.py:144
  50.6 17.3 %all_to_all.30.refs_0_ = f32[4,256,256]{2,1,0:T(8,128)S(1)} all-to-all(f32[4,256,256]{2,1,0:T(8,128)S(1)} %partial_logits.1), channel_id=1, replica_groups=mesh['y'=4,'c'=2,'z'=16,'x'=4] {'x'}, dimensions={0} | all-to-all | bytes 2097152 | tf_op jit(solution)/shard_map/all_to_all | solution.py:322
  67.9 1.0 local_stats.1
  69.0 3.5 %all-to-all-start.2 = ((f32[16,8,128]{2,1,0:T(8,128)}), f32[16,8,128]{2,1,0:T(8,128)S(1)}, u32[]{:S(2)}, u32[]{:S(2)}) async-start(f32[16,8,128]{2,1,0:T(8,128)} %get-tuple-element.8), calls=%async_computation.2 | async-start | bytes 131072 | tf_op jit(solution)/shard_map/all_to_all | solution.py:324
  72.5 3.8 %collective-permute-start.4 = (f32[256,256]{1,0:T(8,128)S(1)}, f32[256,256]{1,0:T(8,128)S(1)}, u32[]{:S(2)}, u32[]{:S(2)}) collective-permute-start(f32[256,256]{1,0:T(8,128)S(1)} %get-tuple-element.9.refs_2_), channel_id=1, source_target_pairs={{3,0},{0,1},{1,2},{2,3},{7,4},{4,5},{5,6},{6,7},{11,8},{8,9},{9,10... | collective-permute-start | bytes 786440 | tf_op jit(solution)/shard_map/ppermute | solution.py:102
  76.3 4.6 %collective-permute-start.3 = (f32[256,256]{1,0:T(8,128)S(1)}, f32[256,256]{1,0:T(8,128)}, u32[]{:S(2)}, u32[]{:S(2)}) collective-permute-start(f32[256,256]{1,0:T(8,128)S(1)} %get-tuple-element.9.refs_2_), channel_id=1, source_target_pairs={{2,0},{3,1},{0,2},{1,3},{6,4},{7,5},{4,6},{5,7},{10,8},{11,9},{8,1... | collective-permute-start | bytes 786440 | tf_op jit(solution)/shard_map/ppermute | solution.py:102
  80.9 3.4 %collective-permute-start.2 = (f32[256,256]{1,0:T(8,128)S(1)}, f32[256,256]{1,0:T(8,128)}, u32[]{:S(2)}, u32[]{:S(2)}) collective-permute-start(f32[256,256]{1,0:T(8,128)S(1)} %get-tuple-element.9.refs_2_), channel_id=1, source_target_pairs={{1,0},{2,1},{3,2},{0,3},{5,4},{6,5},{7,6},{4,7},{9,8},{10,9},{11,1... | collective-permute-start | bytes 786440 | tf_op jit(solution)/shard_map/ppermute | solution.py:102
  84.3 0.7 merged_stats.1
  85.0 6.3 %all-to-all-start.3 = ((f32[16,8,128]{2,1,0:T(8,128)}), f32[16,8,128]{2,1,0:T(8,128)S(1)}, u32[]{:S(2)}, u32[]{:S(2)}) async-start(f32[16,8,128]{2,1,0:T(8,128)} %merged_stats.1), calls=%async_computation.3 | async-start | bytes 131072 | tf_op jit(solution)/shard_map/all_to_all | solution.py:326
  91.3 11.8 %all-to-all-done.3.refs_0_.stats_ref = f32[16,8,128]{2,1,0:T(8,128)S(1)} async-done(((f32[16,8,128]{2,1,0:T(8,128)}), f32[16,8,128]{2,1,0:T(8,128)S(1)}, u32[]{:S(2)}, u32[]{:S(2)}) %all-to-all-start.3) | async-done | bytes 65568 | tf_op jit(solution)/shard_map/all_to_all | solution.py:326
  103.1 2.8 %partial_grad.1 = bf16[256,1792]{1,0:T(8,128)(2,1)S(1)} custom-call(f32[16,8,128]{2,1,0:T(8,128)S(1)} %all-to-all-done.3.refs_0_.stats_ref, f32[8,256]{1,0:T(8,128)S(1)} %row_meta.1.refs_1_.meta_ref, f32[256,256]{1,0:T(8,128)S(1)} %get-tuple-element.9.refs_2_, f32[256,256]{1,0:T(8,128)} %collective-permute-done.2.refs_3_, ...), custom_call_target="tpu_custom_call" | custom-call | flops 939524096 | bytes 1048576 | tf_op jit(solution)/shard_map/partial_grad/pallas_call | solution.py:282
  105.9 14.2 %all_to_all.31 = bf16[4,64,1792]{2,1,0:T(8,128)(2,1)S(1)} all-to-all(bf16[4,64,1792]{2,1,0:T(8,128)(2,1)S(1)} %bitcast.2), channel_id=1, replica_groups=mesh['y'=4,'c'=2,'z'=16,'x'=4] {'y'}, dimensions={0} | all-to-all | bytes 1835008 | tf_op jit(solution)/shard_map/all_to_all | solution.py:329
  120.1 0.2 reduce_sum.24
  120.3 0.8 reshape.20
  121.1 4.4 %all-to-all-start.5 = ((bf16[16,4,1792]{2,1,0:T(4,128)(2,1)}), bf16[16,4,1792]{2,1,0:T(4,128)(2,1)S(1)}, u32[]{:S(2)}, u32[]{:S(2)}) async-start(bf16[16,4,1792]{2,1,0:T(4,128)(2,1)} %reshape.20), calls=%async_computation.5 | async-start | bytes 458752 | tf_op jit(solution)/shard_map/all_to_all | solution.py:331
  125.5 0.7 rows_loss.1
  126.1 1.9 %collective-permute-start.5 = (f32[]{:T(128)}, f32[]{:T(128)}, u32[]{:S(2)}, u32[]{:S(2)}) collective-permute-start(f32[]{:T(128)} %bitcast.1), channel_id=1, source_target_pairs={{0,64},{64,0},{1,65},{65,1},{2,66},{66,2},{3,67},{67,3},{4,68},{68... | collective-permute-start | bytes 20 | tf_op jit(solution)/shard_map/ppermute | solution.py:334
  128.1 1.2 collective-permute-done.5
  130.6 9.2 %all-to-all-done.5 = bf16[16,4,1792]{2,1,0:T(4,128)(2,1)S(1)} async-done(((bf16[16,4,1792]{2,1,0:T(4,128)(2,1)}), bf16[16,4,1792]{2,1,0:T(4,128)(2,1)S(1)}, u32[]{:S(2)}, u32[]{:S(2)}) %all-to-all-start.5) | async-done | bytes 229408 | tf_op jit(solution)/shard_map/all_to_all | solution.py:331
  139.8 0.7 reduce_sum.25
  (19 shorter events, 0.1 us)
Async XLA Ops:
  2.1 32.1 %all-to-all-start = ((bf16[16,4,1792]{2,1,0:T(4,128)(2,1)}), bf16[16,4,1792]{2,1,0:T(4,128)(2,1)S(1)}, u32[]{:S(2)}, u32[]{:S(2)}) async-start(bf16[16,4,1792]{2,1,0:T(4,128)(2,1)} %broadcast_in_dim.2), calls=%async_computation | async-start | bytes 458752 | tf_op jit(solution)/shard_map/all_to_all | solution.py:98
  17.3 7.4 %copy-start.5 = (s32[512]{0:T(512)S(1)}, s32[512]{0:T(512)}, u32[]{:S(2)}) copy-start(s32[512]{0:T(512)} %param.9) | copy-start | bytes 6148
  17.3 7.6 %copy-start.1 = (s32[32]{0:T(128)S(1)}, s32[32]{0:T(128)}, u32[]{:S(2)}) copy-start(s32[32]{0:T(128)} %offsets.1) | copy-start | bytes 388
  17.3 7.6 %copy-start.2 = (s32[32]{0:T(128)S(1)}, s32[32]{0:T(128)}, u32[]{:S(2)}) copy-start(s32[32]{0:T(128)} %lengths.1) | copy-start | bytes 388
  17.4 7.6 %copy-start.3 = (s32[32]{0:T(128)S(1)}, s32[32]{0:T(128)}, u32[]{:S(2)}) copy-start(s32[32]{0:T(128)} %groups.1) | copy-start | bytes 388
  17.4 7.5 %copy-start.4 = (f32[32]{0:T(128)S(1)}, f32[32]{0:T(128)}, u32[]{:S(2)}) copy-start(f32[32]{0:T(128)} %rewards.1) | copy-start | bytes 388
  17.4 31.4 %copy-start = (bf16[1792,512]{1,0:T(8,128)(2,1)S(1)}, bf16[1792,512]{1,0:T(8,128)(2,1)}, u32[]{:S(2)}) copy-start(bf16[1792,512]{1,0:T(8,128)(2,1)} %refs_6_.1) | copy-start | bytes 5505028
  20.4 28.4 %collective-permute-start.1 = (bf16[896,512]{1,0:T(8,128)(2,1)}, bf16[896,512]{1,0:T(8,128)(2,1)S(1)}, u32[]{:S(2)}, u32[]{:S(2)}) collective-permute-start(bf16[896,512]{1,0:T(8,128)(2,1)} %get-tuple-element.10), channel_id=1, source_target_pairs={{0,64},{64,0},{1,65},{65,1},{2,66},{66,2},{3,67},{67,3},{4,68},{68... | collective-permute-start | bytes 2752520 | tf_op jit(solution)/shard_map/ppermute | solution.py:317
  22.3 26.5 %collective-permute-start = (bf16[896,512]{1,0:T(8,128)(2,1)}, bf16[896,512]{1,0:T(8,128)(2,1)}, u32[]{:S(2)}, u32[]{:S(2)}) collective-permute-start(bf16[896,512]{1,0:T(8,128)(2,1)} %get-tuple-element.11), channel_id=1, source_target_pairs={{0,64},{64,0},{1,65},{65,1},{2,66},{66,2},{3,67},{67,3},{4,68},{68... | collective-permute-start | bytes 2752520 | tf_op jit(solution)/shard_map/ppermute | solution.py:317
  69.0 15.3 %all-to-all-start.2 = ((f32[16,8,128]{2,1,0:T(8,128)}), f32[16,8,128]{2,1,0:T(8,128)S(1)}, u32[]{:S(2)}, u32[]{:S(2)}) async-start(f32[16,8,128]{2,1,0:T(8,128)} %get-tuple-element.8), calls=%async_computation.2 | async-start | bytes 131072 | tf_op jit(solution)/shard_map/all_to_all | solution.py:324
  72.5 18.8 %collective-permute-start.4 = (f32[256,256]{1,0:T(8,128)S(1)}, f32[256,256]{1,0:T(8,128)S(1)}, u32[]{:S(2)}, u32[]{:S(2)}) collective-permute-start(f32[256,256]{1,0:T(8,128)S(1)} %get-tuple-element.9.refs_2_), channel_id=1, source_target_pairs={{3,0},{0,1},{1,2},{2,3},{7,4},{4,5},{5,6},{6,7},{11,8},{8,9},{9,10... | collective-permute-start | bytes 786440 | tf_op jit(solution)/shard_map/ppermute | solution.py:102
  76.3 15.0 %collective-permute-start.3 = (f32[256,256]{1,0:T(8,128)S(1)}, f32[256,256]{1,0:T(8,128)}, u32[]{:S(2)}, u32[]{:S(2)}) collective-permute-start(f32[256,256]{1,0:T(8,128)S(1)} %get-tuple-element.9.refs_2_), channel_id=1, source_target_pairs={{2,0},{3,1},{0,2},{1,3},{6,4},{7,5},{4,6},{5,7},{10,8},{11,9},{8,1... | collective-permute-start | bytes 786440 | tf_op jit(solution)/shard_map/ppermute | solution.py:102
  80.9 10.4 %collective-permute-start.2 = (f32[256,256]{1,0:T(8,128)S(1)}, f32[256,256]{1,0:T(8,128)}, u32[]{:S(2)}, u32[]{:S(2)}) collective-permute-start(f32[256,256]{1,0:T(8,128)S(1)} %get-tuple-element.9.refs_2_), channel_id=1, source_target_pairs={{1,0},{2,1},{3,2},{0,3},{5,4},{6,5},{7,6},{4,7},{9,8},{10,9},{11,1... | collective-permute-start | bytes 786440 | tf_op jit(solution)/shard_map/ppermute | solution.py:102
  85.0 18.1 %all-to-all-start.3 = ((f32[16,8,128]{2,1,0:T(8,128)}), f32[16,8,128]{2,1,0:T(8,128)S(1)}, u32[]{:S(2)}, u32[]{:S(2)}) async-start(f32[16,8,128]{2,1,0:T(8,128)} %merged_stats.1), calls=%async_computation.3 | async-start | bytes 131072 | tf_op jit(solution)/shard_map/all_to_all | solution.py:326
  121.1 18.7 %all-to-all-start.5 = ((bf16[16,4,1792]{2,1,0:T(4,128)(2,1)}), bf16[16,4,1792]{2,1,0:T(4,128)(2,1)S(1)}, u32[]{:S(2)}, u32[]{:S(2)}) async-start(bf16[16,4,1792]{2,1,0:T(4,128)(2,1)} %reshape.20), calls=%async_computation.5 | async-start | bytes 458752 | tf_op jit(solution)/shard_map/all_to_all | solution.py:331
  126.1 3.1 %collective-permute-start.5 = (f32[]{:T(128)}, f32[]{:T(128)}, u32[]{:S(2)}, u32[]{:S(2)}) collective-permute-start(f32[]{:T(128)} %bitcast.1), channel_id=1, source_target_pairs={{0,64},{64,0},{1,65},{65,1},{2,66},{66,2},{3,67},{67,3},{4,68},{68... | collective-permute-start | bytes 20 | tf_op jit(solution)/shard_map/ppermute | solution.py:334

commit v7 on v6

--- a/solution.py
+++ b/solution.py
@@ -8,7 +8,6 @@
 GROUP_SIZE = 16
 GROUPS = 2
 ENTROPY_WEIGHT = 0.2
-STEP = 256
 Y, C, Z, X = 4, 2, 16, 4
 VMEM = pl.BlockSpec(memory_space=pltpu.VMEM)
 ANY = pl.BlockSpec(memory_space=pl.ANY)
@@ -232,7 +231,7 @@
 
 
 def grad_kernel(vocab, stats_ref, meta_ref, l0, l1, l2, l3, own_ref, *refs):
-    *other_hbm, out_ref, g_ref, acc_ref, other_ref, l_ref, sem, move_sem = refs
+    *other_hbm, out_ref, other_ref, l_ref, sem, move_sem = refs
     x = lax.axis_index("x")
     moves = [
         pltpu.make_async_copy(ref, l_ref.at[lax.rem(x + k, X)], move_sem.at[k])
@@ -251,29 +250,27 @@
     width = l0.shape[1]
     for copy in moves:
         copy.wait()
-    for chunk in range(X):
-        log_probability = l_ref[chunk] - log_total
-        probability = jnp.exp(log_probability)
-        column = lax.broadcasted_iota(jnp.int32, (n, width), 1) + first_column(chunk, vocab, width)
-        hit = jnp.where(column == target, 1.0, 0.0)
-        grad = row_weight * (
-            advantage * (probability - hit)
-            + ENTROPY_WEIGHT * probability * (log_probability + entropy)
-        )
-        g_ref[:, chunk * width : (chunk + 1) * width] = grad.astype(jnp.bfloat16)
+
+    def core_grad(first):
+        parts = []
+        for chunk in range(first, first + X // C):
+            log_probability = l_ref[chunk] - log_total
+            probability = jnp.exp(log_probability)
+            column = lax.broadcasted_iota(jnp.int32, (n, width), 1) + first_column(chunk, vocab, width)
+            hit = jnp.where(column == target, 1.0, 0.0)
+            grad = row_weight * (
+                advantage * (probability - hit)
+                + ENTROPY_WEIGHT * probability * (log_probability + entropy)
+            )
+            parts.append(grad.astype(jnp.bfloat16))
+        return jnp.concatenate(parts, axis=1)
+
     contract = (((1,), (1,)), ((), ()))
-    depth = own_ref.shape[0]
-    for at in range(0, depth, STEP):
-        acc_ref[:, at : at + STEP] = lax.dot_general(
-            g_ref[:, :vocab], own_ref[at : at + STEP], contract, preferred_element_type=jnp.float32
-        )
+    own = lax.dot_general(core_grad(0), own_ref[...], contract, preferred_element_type=jnp.float32)
     for copy in fetch:
         copy.wait()
-    for at in range(0, depth, STEP):
-        part = acc_ref[:, at : at + STEP] + lax.dot_general(
-            g_ref[:, vocab:], other_ref[at : at + STEP], contract, preferred_element_type=jnp.float32
-        )
-        out_ref[:, at : at + STEP] = part.astype(jnp.bfloat16)
+    other = lax.dot_general(core_grad(X // C), other_ref[...], contract, preferred_element_type=jnp.float32)
+    out_ref[...] = (own + other).astype(jnp.bfloat16)
 
 
 def partial_grad(stats, meta, chunks, own, other):
@@ -285,8 +282,6 @@
         in_specs=[VMEM] * 2 + [ANY] * X + [VMEM] + [ANY] * len(other),
         out_specs=VMEM,
         scratch_shapes=[
-            pltpu.VMEM((n, C * vocab), jnp.bfloat16),
-            pltpu.VMEM((n, depth), jnp.float32),
             pltpu.VMEM(own.shape, own.dtype),
             pltpu.VMEM((X, n, width), jnp.float32),
             pltpu.SemaphoreType.DMA((len(other),)),

time: 142 us -> 142 us (level)
  no operation moved by 1% of the time
where the time goes in v7:
time: 142 us; the launch traced here: 141 us
  starting transfers between devices  47.4 us (33%)
  blocking collectives  46 us (32%)
  waiting for transfers between devices  30.8 us (22%)
  Pallas kernels  7.65 us (5%)
  local copies, waits for them, and re-layouts  5.49 us (4%)
  between operations  3.28 us (2%)
    all_to_all x1, blocking collectives, per_device(): part = lax.all_to_all(part, 'x', 0, 0, tiled=True)  17.3 us
    all_to_all x1, starting transfers between devices, spread(): return lax.all_to_all(sent, axes, 0, 0, tiled=True)  15.2 us
    all_gather x1, blocking collectives, per_device(): my_rows = lax.all_gather(tok_rows, 'y', axis=0, tiled=True)  14.5 us
    all_to_all x1, blocking collectives, per_device(): lax.all_to_all(hidden_grad.reshape(Y, per_tok, depth), 'y', 0, 0, tiled=T...  14.2 us
    all_to_all x1, waiting for transfers between devices, per_device(): stats = lax.all_to_all(merged_stats(stats, Z), 'z', 0, 0, tiled=True)  11.8 us
    ppermute x3, starting transfers between devices, x_neighbour(): return lax.ppermute(block, 'x', [((i + k) % X, i) for i in range(X)])  11.8 us
    all_to_all x1, waiting for transfers between devices, per_device(): lax.all_to_all(hidden_grad.reshape(Z, per_tok // Z, depth), 'z', 0, 0, ti...  9.23 us
    all_to_all x1, waiting for transfers between devices, spread(): return lax.all_to_all(sent, axes, 0, 0, tiled=True)  8.54 us
  transfers between devices with their start and end apart: 10, of which 4 were waited for; matrix products, arithmetic and copies ran while one was open for 2% of the time, Pallas kernels for 1%

profile of v7, /device:TPU:32, one launch (start us, length us, event | category | flops | bytes accessed | tf_op | source)
XLA Modules:
  0.0 141.5 jit_solution(13853738606473093833)
XLA Ops:
  0.6 1.5 %broadcast_in_dim.2 = bf16[16,4,1792]{2,1,0:T(4,128)(2,1)} broadcast(bf16[4,1792]{1,0:T(4,128)(2,1)} %param.7), dimensions={1,2} | broadcast | bytes 243712 | tf_op jit(solution)/shard_map/broadcast_in_dim | solution.py:96
  2.1 15.2 %all-to-all-start = ((bf16[16,4,1792]{2,1,0:T(4,128)(2,1)}), bf16[16,4,1792]{2,1,0:T(4,128)(2,1)S(1)}, u32[]{:S(2)}, u32[]{:S(2)}) async-start(bf16[16,4,1792]{2,1,0:T(4,128)(2,1)} %broadcast_in_dim.2), calls=%async_computation | async-start | bytes 458752 | tf_op jit(solution)/shard_map/all_to_all | solution.py:97
  17.3 0.0 copy-start.1
  17.4 3.0 %fusion = (bf16[896,512]{1,0:T(8,128)(2,1)}, bf16[896,512]{1,0:T(8,128)(2,1)}) fusion(bf16[1792,512]{1,0:T(8,128)(2,1)} %refs_6_.1), kind=kLoop, calls=%fused_computation.1 | loop fusion | bytes 3670016 | tf_op jit(solution)/shard_map/split | solution.py:312
  20.4 1.9 %collective-permute-start.1 = (bf16[896,512]{1,0:T(8,128)(2,1)}, bf16[896,512]{1,0:T(8,128)(2,1)S(1)}, u32[]{:S(2)}, u32[]{:S(2)}) collective-permute-start(bf16[896,512]{1,0:T(8,128)(2,1)} %get-tuple-element.10), channel_id=1, source_target_pairs={{0,64},{64,0},{1,65},{65,1},{2,66},{66,2},{3,67},{67,3},{4,68},{68... | collective-permute-start | bytes 2752520 | tf_op jit(solution)/shard_map/ppermute | solution.py:312
  22.3 2.4 %collective-permute-start = (bf16[896,512]{1,0:T(8,128)(2,1)}, bf16[896,512]{1,0:T(8,128)(2,1)}, u32[]{:S(2)}, u32[]{:S(2)}) collective-permute-start(bf16[896,512]{1,0:T(8,128)(2,1)} %get-tuple-element.11), channel_id=1, source_target_pairs={{0,64},{64,0},{1,65},{65,1},{2,66},{66,2},{3,67},{67,3},{4,68},{68... | collective-permute-start | bytes 2752520 | tf_op jit(solution)/shard_map/ppermute | solution.py:312
  24.7 0.1 reshape.18
  24.8 0.1 reshape_squeeze.3.target_ref
  24.9 0.8 row_meta.1.refs_1_.meta_ref
  25.7 8.5 %all-to-all-done = bf16[16,4,1792]{2,1,0:T(4,128)(2,1)S(1)} async-done(((bf16[16,4,1792]{2,1,0:T(4,128)(2,1)}), bf16[16,4,1792]{2,1,0:T(4,128)(2,1)S(1)}, u32[]{:S(2)}, u32[]{:S(2)}) %all-to-all-start) | async-done | bytes 229408 | tf_op jit(solution)/shard_map/all_to_all | solution.py:97
  34.2 0.1 reshape.17
  34.3 14.5 %all_gather.3.rows_ref = bf16[256,1792]{1,0:T(8,128)(2,1)S(1)} all-gather(bf16[64,1792]{1,0:T(8,128)(2,1)S(1)} %reshape.17), channel_id=1, replica_groups=mesh['y'=4,'c'=2,'z'=16,'x'=4] {'y'}, dimensions={0}, use_global_device_ids=true | all-gather | bytes 1146880 | tf_op jit(solution)/shard_map/all_gather | solution.py:314
  48.8 1.8 %partial_logits.1 = f32[4,256,256]{2,1,0:T(8,128)S(1)} custom-call(bf16[256,1792]{1,0:T(8,128)(2,1)S(1)} %all_gather.3.rows_ref, bf16[1792,512]{1,0:T(8,128)(2,1)S(1)} %copy-done, bf16[896,512]{1,0:T(8,128)(2,1)} %collective-permute-done.refs_0_.refs_7_, bf16[896,512]{1,0:T(8,128)(2,1)S(1)} %collective-permute-done.1.refs_1_.refs_8_), custom_call_target="tpu_custom_call" | custom-call | flops 939524096 | bytes 1048576 | tf_op jit(solution)/shard_map/partial_logits/pallas_call | solution.py:143
  50.6 17.3 %all_to_all.30.refs_0_ = f32[4,256,256]{2,1,0:T(8,128)S(1)} all-to-all(f32[4,256,256]{2,1,0:T(8,128)S(1)} %partial_logits.1), channel_id=1, replica_groups=mesh['y'=4,'c'=2,'z'=16,'x'=4] {'x'}, dimensions={0} | all-to-all | bytes 2097152 | tf_op jit(solution)/shard_map/all_to_all | solution.py:317
  67.9 1.0 local_stats.1
  69.0 3.5 %all-to-all-start.2 = ((f32[16,8,128]{2,1,0:T(8,128)}), f32[16,8,128]{2,1,0:T(8,128)S(1)}, u32[]{:S(2)}, u32[]{:S(2)}) async-start(f32[16,8,128]{2,1,0:T(8,128)} %get-tuple-element.8), calls=%async_computation.2 | async-start | bytes 131072 | tf_op jit(solution)/shard_map/all_to_all | solution.py:319
  72.5 3.8 %collective-permute-start.4 = (f32[256,256]{1,0:T(8,128)S(1)}, f32[256,256]{1,0:T(8,128)S(1)}, u32[]{:S(2)}, u32[]{:S(2)}) collective-permute-start(f32[256,256]{1,0:T(8,128)S(1)} %get-tuple-element.9.refs_2_), channel_id=1, source_target_pairs={{3,0},{0,1},{1,2},{2,3},{7,4},{4,5},{5,6},{6,7},{11,8},{8,9},{9,10... | collective-permute-start | bytes 786440 | tf_op jit(solution)/shard_map/ppermute | solution.py:101
  76.3 4.6 %collective-permute-start.3 = (f32[256,256]{1,0:T(8,128)S(1)}, f32[256,256]{1,0:T(8,128)}, u32[]{:S(2)}, u32[]{:S(2)}) collective-permute-start(f32[256,256]{1,0:T(8,128)S(1)} %get-tuple-element.9.refs_2_), channel_id=1, source_target_pairs={{2,0},{3,1},{0,2},{1,3},{6,4},{7,5},{4,6},{5,7},{10,8},{11,9},{8,1... | collective-permute-start | bytes 786440 | tf_op jit(solution)/shard_map/ppermute | solution.py:101
  80.9 3.4 %collective-permute-start.2 = (f32[256,256]{1,0:T(8,128)S(1)}, f32[256,256]{1,0:T(8,128)}, u32[]{:S(2)}, u32[]{:S(2)}) collective-permute-start(f32[256,256]{1,0:T(8,128)S(1)} %get-tuple-element.9.refs_2_), channel_id=1, source_target_pairs={{1,0},{2,1},{3,2},{0,3},{5,4},{6,5},{7,6},{4,7},{9,8},{10,9},{11,1... | collective-permute-start | bytes 786440 | tf_op jit(solution)/shard_map/ppermute | solution.py:101
  84.3 0.7 merged_stats.1
  85.0 6.3 %all-to-all-start.3 = ((f32[16,8,128]{2,1,0:T(8,128)}), f32[16,8,128]{2,1,0:T(8,128)S(1)}, u32[]{:S(2)}, u32[]{:S(2)}) async-start(f32[16,8,128]{2,1,0:T(8,128)} %merged_stats.1), calls=%async_computation.3 | async-start | bytes 131072 | tf_op jit(solution)/shard_map/all_to_all | solution.py:321
  91.3 11.8 %all-to-all-done.3.refs_0_.stats_ref = f32[16,8,128]{2,1,0:T(8,128)S(1)} async-done(((f32[16,8,128]{2,1,0:T(8,128)}), f32[16,8,128]{2,1,0:T(8,128)S(1)}, u32[]{:S(2)}, u32[]{:S(2)}) %all-to-all-start.3) | async-done | bytes 65568 | tf_op jit(solution)/shard_map/all_to_all | solution.py:321
  103.1 2.7 %partial_grad.1 = bf16[256,1792]{1,0:T(8,128)(2,1)S(1)} custom-call(f32[16,8,128]{2,1,0:T(8,128)S(1)} %all-to-all-done.3.refs_0_.stats_ref, f32[8,256]{1,0:T(8,128)S(1)} %row_meta.1.refs_1_.meta_ref, f32[256,256]{1,0:T(8,128)S(1)} %get-tuple-element.9.refs_2_, f32[256,256]{1,0:T(8,128)} %collective-permute-done.2.refs_3_, ...), custom_call_target="tpu_custom_call" | custom-call | flops 939524096 | bytes 1048576 | tf_op jit(solution)/shard_map/partial_grad/pallas_call | solution.py:279
  105.8 14.2 %all_to_all.31 = bf16[4,64,1792]{2,1,0:T(8,128)(2,1)S(1)} all-to-all(bf16[4,64,1792]{2,1,0:T(8,128)(2,1)S(1)} %bitcast.2), channel_id=1, replica_groups=mesh['y'=4,'c'=2,'z'=16,'x'=4] {'y'}, dimensions={0} | all-to-all | bytes 1835008 | tf_op jit(solution)/shard_map/all_to_all | solution.py:324
  120.0 0.2 reduce_sum.24
  120.1 0.8 reshape.20
  120.9 4.4 %all-to-all-start.5 = ((bf16[16,4,1792]{2,1,0:T(4,128)(2,1)}), bf16[16,4,1792]{2,1,0:T(4,128)(2,1)S(1)}, u32[]{:S(2)}, u32[]{:S(2)}) async-start(bf16[16,4,1792]{2,1,0:T(4,128)(2,1)} %reshape.20), calls=%async_computation.5 | async-start | bytes 458752 | tf_op jit(solution)/shard_map/all_to_all | solution.py:326
  125.3 0.7 rows_loss.1
  126.0 1.9 %collective-permute-start.5 = (f32[]{:T(128)}, f32[]{:T(128)}, u32[]{:S(2)}, u32[]{:S(2)}) collective-permute-start(f32[]{:T(128)} %bitcast.1), channel_id=1, source_target_pairs={{0,64},{64,0},{1,65},{65,1},{2,66},{66,2},{3,67},{67,3},{4,68},{68... | collective-permute-start | bytes 20 | tf_op jit(solution)/shard_map/ppermute | solution.py:329
  127.9 1.2 collective-permute-done.5
  130.4 9.2 %all-to-all-done.5 = bf16[16,4,1792]{2,1,0:T(4,128)(2,1)S(1)} async-done(((bf16[16,4,1792]{2,1,0:T(4,128)(2,1)}), bf16[16,4,1792]{2,1,0:T(4,128)(2,1)S(1)}, u32[]{:S(2)}, u32[]{:S(2)}) %all-to-all-start.5) | async-done | bytes 229408 | tf_op jit(solution)/shard_map/all_to_all | solution.py:326
  139.6 0.7 reduce_sum.25
  (19 shorter events, 0.1 us)
Async XLA Ops:
  2.1 32.1 %all-to-all-start = ((bf16[16,4,1792]{2,1,0:T(4,128)(2,1)}), bf16[16,4,1792]{2,1,0:T(4,128)(2,1)S(1)}, u32[]{:S(2)}, u32[]{:S(2)}) async-start(bf16[16,4,1792]{2,1,0:T(4,128)(2,1)} %broadcast_in_dim.2), calls=%async_computation | async-start | bytes 458752 | tf_op jit(solution)/shard_map/all_to_all | solution.py:97
  17.3 7.4 %copy-start.5 = (s32[512]{0:T(512)S(1)}, s32[512]{0:T(512)}, u32[]{:S(2)}) copy-start(s32[512]{0:T(512)} %param.9) | copy-start | bytes 6148
  17.3 7.6 %copy-start.1 = (s32[32]{0:T(128)S(1)}, s32[32]{0:T(128)}, u32[]{:S(2)}) copy-start(s32[32]{0:T(128)} %offsets.1) | copy-start | bytes 388
  17.3 7.6 %copy-start.2 = (s32[32]{0:T(128)S(1)}, s32[32]{0:T(128)}, u32[]{:S(2)}) copy-start(s32[32]{0:T(128)} %lengths.1) | copy-start | bytes 388
  17.4 7.6 %copy-start.3 = (s32[32]{0:T(128)S(1)}, s32[32]{0:T(128)}, u32[]{:S(2)}) copy-start(s32[32]{0:T(128)} %groups.1) | copy-start | bytes 388
  17.4 7.5 %copy-start.4 = (f32[32]{0:T(128)S(1)}, f32[32]{0:T(128)}, u32[]{:S(2)}) copy-start(f32[32]{0:T(128)} %rewards.1) | copy-start | bytes 388
  17.4 31.4 %copy-start = (bf16[1792,512]{1,0:T(8,128)(2,1)S(1)}, bf16[1792,512]{1,0:T(8,128)(2,1)}, u32[]{:S(2)}) copy-start(bf16[1792,512]{1,0:T(8,128)(2,1)} %refs_6_.1) | copy-start | bytes 5505028
  20.4 28.4 %collective-permute-start.1 = (bf16[896,512]{1,0:T(8,128)(2,1)}, bf16[896,512]{1,0:T(8,128)(2,1)S(1)}, u32[]{:S(2)}, u32[]{:S(2)}) collective-permute-start(bf16[896,512]{1,0:T(8,128)(2,1)} %get-tuple-element.10), channel_id=1, source_target_pairs={{0,64},{64,0},{1,65},{65,1},{2,66},{66,2},{3,67},{67,3},{4,68},{68... | collective-permute-start | bytes 2752520 | tf_op jit(solution)/shard_map/ppermute | solution.py:312
  22.3 26.5 %collective-permute-start = (bf16[896,512]{1,0:T(8,128)(2,1)}, bf16[896,512]{1,0:T(8,128)(2,1)}, u32[]{:S(2)}, u32[]{:S(2)}) collective-permute-start(bf16[896,512]{1,0:T(8,128)(2,1)} %get-tuple-element.11), channel_id=1, source_target_pairs={{0,64},{64,0},{1,65},{65,1},{2,66},{66,2},{3,67},{67,3},{4,68},{68... | collective-permute-start | bytes 2752520 | tf_op jit(solution)/shard_map/ppermute | solution.py:312
  69.0 15.3 %all-to-all-start.2 = ((f32[16,8,128]{2,1,0:T(8,128)}), f32[16,8,128]{2,1,0:T(8,128)S(1)}, u32[]{:S(2)}, u32[]{:S(2)}) async-start(f32[16,8,128]{2,1,0:T(8,128)} %get-tuple-element.8), calls=%async_computation.2 | async-start | bytes 131072 | tf_op jit(solution)/shard_map/all_to_all | solution.py:319
  72.5 18.8 %collective-permute-start.4 = (f32[256,256]{1,0:T(8,128)S(1)}, f32[256,256]{1,0:T(8,128)S(1)}, u32[]{:S(2)}, u32[]{:S(2)}) collective-permute-start(f32[256,256]{1,0:T(8,128)S(1)} %get-tuple-element.9.refs_2_), channel_id=1, source_target_pairs={{3,0},{0,1},{1,2},{2,3},{7,4},{4,5},{5,6},{6,7},{11,8},{8,9},{9,10... | collective-permute-start | bytes 786440 | tf_op jit(solution)/shard_map/ppermute | solution.py:101
  76.3 15.0 %collective-permute-start.3 = (f32[256,256]{1,0:T(8,128)S(1)}, f32[256,256]{1,0:T(8,128)}, u32[]{:S(2)}, u32[]{:S(2)}) collective-permute-start(f32[256,256]{1,0:T(8,128)S(1)} %get-tuple-element.9.refs_2_), channel_id=1, source_target_pairs={{2,0},{3,1},{0,2},{1,3},{6,4},{7,5},{4,6},{5,7},{10,8},{11,9},{8,1... | collective-permute-start | bytes 786440 | tf_op jit(solution)/shard_map/ppermute | solution.py:101
  80.9 10.4 %collective-permute-start.2 = (f32[256,256]{1,0:T(8,128)S(1)}, f32[256,256]{1,0:T(8,128)}, u32[]{:S(2)}, u32[]{:S(2)}) collective-permute-start(f32[256,256]{1,0:T(8,128)S(1)} %get-tuple-element.9.refs_2_), channel_id=1, source_target_pairs={{1,0},{2,1},{3,2},{0,3},{5,4},{6,5},{7,6},{4,7},{9,8},{10,9},{11,1... | collective-permute-start | bytes 786440 | tf_op jit(solution)/shard_map/ppermute | solution.py:101
  85.0 18.1 %all-to-all-start.3 = ((f32[16,8,128]{2,1,0:T(8,128)}), f32[16,8,128]{2,1,0:T(8,128)S(1)}, u32[]{:S(2)}, u32[]{:S(2)}) async-start(f32[16,8,128]{2,1,0:T(8,128)} %merged_stats.1), calls=%async_computation.3 | async-start | bytes 131072 | tf_op jit(solution)/shard_map/all_to_all | solution.py:321
  120.9 18.7 %all-to-all-start.5 = ((bf16[16,4,1792]{2,1,0:T(4,128)(2,1)}), bf16[16,4,1792]{2,1,0:T(4,128)(2,1)S(1)}, u32[]{:S(2)}, u32[]{:S(2)}) async-start(bf16[16,4,1792]{2,1,0:T(4,128)(2,1)} %reshape.20), calls=%async_computation.5 | async-start | bytes 458752 | tf_op jit(solution)/shard_map/all_to_all | solution.py:326
  126.0 3.1 %collective-permute-start.5 = (f32[]{:T(128)}, f32[]{:T(128)}, u32[]{:S(2)}, u32[]{:S(2)}) collective-permute-start(f32[]{:T(128)} %bitcast.1), channel_id=1, source_target_pairs={{0,64},{64,0},{1,65},{65,1},{2,66},{66,2},{3,67},{67,3},{4,68},{68... | collective-permute-start | bytes 20 | tf_op jit(solution)/shard_map/ppermute | solution.py:329
